TPU v7x, 128 devices: a whole 4x4x4 slice. The times are simulated.
128 devices in a mesh: row: 16 (over z, y), col: 8 (over x, core).
Axes of the slice: x: 4, y: 4, z: 4, core: 2. Of those that a mesh axis runs over, the one named last changes fastest.
Arguments:
- inputs: bfloat16 [4, 16, 256, 768], P(None, 'row', 'col'), may hold values from -6 to 6
- panel_order: int32 [2], replicated, may hold values from 0 to 63, as said below
Outputs:
- factor_panels: float32 [4, 16, 256, 512], P(None, 'row')
- trailing: float32 [4, 16, 256, 8, 8, 256], P(None, 'row', None, None, 'col')
Inputs may be any that keep to these rules, and one draw needn't show every extreme that they name: `panel_order`: 2 distinct tile indices, the last tile 64 - 1 always among them.
All inputs are finite; a program needn't handle non-finite values.
Results may differ from a plain program's by a relative error of at most 0.0003.
Values may be sent and summed in bfloat16 or wider, within the bound.
No kernel may reach another device: no remote copies, remote signals or barrier semaphores. Data moves between devices by JAX's collectives and lax.ppermute only.
A program may use at most 128 MiB of HBM per device.

v0:
```python
import math

import jax
import jax.numpy as jnp
from jax import lax
from jax.sharding import PartitionSpec as P

D0 = 768
LAYERS = 3
PANELS = 2


weight_variance = 2.0
bias_variance = 0.1
ridge_term = 0.1


def from_root(block, axis, owner):
    block = jnp.where(lax.axis_index(axis) == owner, block, jnp.zeros_like(block))
    return lax.psum(block, axis)


def arc_cosine(kernel, diagonal_rows, diagonal_columns):
    for layer_index in range(LAYERS):
        magnitude = jnp.sqrt(diagonal_rows[:, None] * diagonal_columns[None, :])
        cosine = jnp.clip(kernel / magnitude, -1.0, 1.0)
        theta_angle = jnp.arccos(cosine)
        kernel = bias_variance + weight_variance / (2.0 * math.pi) * magnitude * (
            jnp.sqrt(1.0 - cosine * cosine) + (math.pi - theta_angle) * cosine
        )
        diagonal_rows = 0.5 * weight_variance * diagonal_rows + bias_variance
        diagonal_columns = 0.5 * weight_variance * diagonal_columns + bias_variance
    return kernel


def per_device(inputs, panel_order):
    row_count = lax.axis_size("row")
    column_count = lax.axis_size("col")
    row_ratio = row_count // column_count
    row_position = lax.axis_index("row")
    column_position = lax.axis_index("col")
    row_inputs = lax.all_gather(inputs, "col", axis=2, tiled=True)
    tile_count = row_inputs.shape[0]
    tile_size = row_inputs.shape[2]
    everything = lax.all_gather(row_inputs, "row", axis=1, tiled=True)
    regrouped = everything.reshape(-1, column_count, tile_size, D0)
    column_inputs = lax.dynamic_index_in_dim(regrouped, column_position, 1, keepdims=False)
    column_tiles = column_inputs.shape[0]
    row_flat = row_inputs.reshape(-1, D0)
    column_flat = column_inputs.reshape(-1, D0)
    kernel = jnp.dot(row_flat, column_flat.T, preferred_element_type=jnp.float32) / D0
    diagonal_rows = jnp.sum(jnp.square(row_flat.astype(jnp.float32)), axis=1) / D0
    diagonal_columns = jnp.sum(jnp.square(column_flat.astype(jnp.float32)), axis=1) / D0
    kernel = arc_cosine(kernel, diagonal_rows, diagonal_columns)
    within_tile = jnp.arange(tile_size, dtype=jnp.int32)
    row_numbers = (
        (jnp.arange(tile_count, dtype=jnp.int32)[:, None] * row_count + row_position) * tile_size
        + within_tile[None, :]
    ).reshape(-1)
    column_numbers = (
        (jnp.arange(column_tiles, dtype=jnp.int32)[:, None] * column_count + column_position)
        * tile_size
        + within_tile[None, :]
    ).reshape(-1)
    matrix = kernel + ridge_term * (row_numbers[:, None] == column_numbers[None, :]).astype(
        jnp.float32
    )
    identity_tile = jnp.eye(tile_size, dtype=jnp.float32)
    factors = []
    for panel_index in range(PANELS):
        target = panel_order[panel_index]
        panel_slab = lax.dynamic_slice_in_dim(
            matrix, target // column_count * tile_size, tile_size, 1
        )
        pivot_local = lax.dynamic_slice_in_dim(
            panel_slab, target // row_count * tile_size, tile_size, 0
        )
        pivot_block = from_root(pivot_local, "row", target % row_count)
        holder = column_position == target % column_count
        pivot_block = jnp.where(holder, pivot_block, identity_tile)
        lower_factor = jnp.linalg.cholesky(pivot_block)
        local_factor = lax.linalg.triangular_solve(
            lower_factor, panel_slab, left_side=False, lower=True, transpose_a=True
        )
        row_factor = from_root(local_factor, "col", target % column_count)
        shaped = row_factor.reshape(tile_count, tile_size, tile_size)
        received_panels = [
            from_root(shaped, "row", root_step * column_count + column_position)
            for root_step in range(row_ratio)
        ]
        column_factor = jnp.stack(received_panels, axis=1).reshape(-1, tile_size)
        row_factor, column_factor = (row_factor, column_factor)
        matrix = matrix - jnp.dot(row_factor, column_factor.T, precision=lax.Precision.HIGHEST)
        factors.append(row_factor)
    factor_panels = jnp.concatenate(factors, axis=1).reshape(tile_count, 1, tile_size, -1)
    trailing = matrix.reshape(tile_count, 1, tile_size, column_tiles, 1, tile_size)
    return (factor_panels, trailing)


def solution(mesh):
    in_specs = (P(None, "row", "col", None), P())
    out_specs = (P(None, "row", None, None), P(None, "row", None, None, "col", None))
    return jax.shard_map(
        per_device, mesh=mesh, in_specs=in_specs, out_specs=out_specs, check_vma=False
    )
```

profile of v0, /device:TPU:0, one launch (start us, length us, event | category | flops | bytes accessed | tf_op | source)
XLA Modules:
  0.0 952.8 jit_solution(8311063281257406052)
XLA Ops:
  7.9 28.7 %all-gather.3.cloned.1.call-done = bf16[4,1,256,768]{3,2,1,0:T(8,128)(2,1)} async-done(((bf16[4,1,32,768]{3,2,1,0:T(8,128)(2,1)}), bf16[4,1,256,768]{3,2,1,0:T(8,128)(2,1)}) %all-gather.3.cloned.1.call-update) | async-done | bytes 1572880 | tf_op jit(solution)/shard_map/all_gather | solution.py:42
  40.9 1.8 multiply_reduce_fusion.1
  42.8 150.6 %all-gather.5.cloned.1.call-done = bf16[4,16,256,768]{3,2,1,0:T(8,128)(2,1)} async-done(((bf16[4,1,256,768]{3,2,1,0:T(8,128)(2,1)}), bf16[4,16,256,768]{3,2,1,0:T(8,128)(2,1)}) %all-gather.5.cloned.1.call-update) | async-done | bytes 25165840 | tf_op jit(solution)/shard_map/all_gather | solution.py:45
  193.4 2.6 multiply_reduce_fusion
  196.0 73.0 %select_add_fusion = f32[1024,2048]{0,1:T(8,128)S(1)} fusion(bf16[2048,768]{1,0:T(8,128)(2,1)S(1)} %bitcast.111, bf16[1024,768]{1,0:T(8,128)(2,1)S(1)} %bitcast.104, s32[1024]{0:T(1024)S(1)} %bitcast.119, f32[2048]{0:T(1024)S(1)} %bitcast.115, f32[1024]{0:T(1024)S(1)} %bitcast.117, f32[2048]{0:T(1024)S(1)} %get-tuple-element.63, ...), kind=kOutput, calls=%fused_computation.6 | convolution fusion | flops 3317694464 | bytes 13156352 | tf_op jit(solution)/shard_map/dot_general | solution.py:51
  269.0 3.4 copy-done.1
  273.3 84.1 %all-reduce.10.cloned.1.call-done = f32[256,256]{0,1:T(8,128)} async-done(((f32[256,256]{0,1:T(8,128)}), f32[256,256]{0,1:T(8,128)}) %all-reduce.10.cloned.1.call-update) | async-done | bytes 262160 | tf_op jit(solution)/shard_map/psum | solution.py:20
  357.7 11.7 %cholesky.130 = f32[128,128]{1,0:T(8,128)S(1)} custom-call(f32[128,128]{1,0:T(8,128)S(1)} %cholesky.194), custom_call_target="Cholesky" | custom-call | tf_op jit(solution)/shard_map/jit(cholesky)/cholesky | solution.py:81
  369.4 9.8 %custom-call.13 = f32[1,128,128]{1,2,0:T(8,128)S(1)} custom-call(f32[1,128,128]{2,1,0:T(8,128)S(1)} %get-tuple-element.61), custom_call_target="InvertDiagBlocksLowerTriangular" | custom-call | tf_op jit(solution)/shard_map/jit(cholesky)/cholesky | solution.py:81
  379.7 11.7 %cholesky.147 = f32[128,128]{1,0:T(8,128)S(1)} custom-call(f32[128,128]{1,0:T(8,128)S(1)} %convolution_subtract_fusion.5), custom_call_target="Cholesky" | custom-call | tf_op jit(solution)/shard_map/jit(cholesky)/cholesky | solution.py:81
  393.6 4.2 while.4
  397.8 19.7 %custom-call.14 = f32[2,128,128]{1,2,0:T(8,128)S(1)} custom-call(f32[2,128,128]{2,1,0:T(8,128)S(1)} %get-tuple-element.18), custom_call_target="InvertDiagBlocksLowerTriangular" | custom-call | tf_op jit(solution)/shard_map/triangular_solve/custom-call.0 | solution.py:82
  422.6 61.6 %all-reduce.12.cloned.1.call-done = f32[1024,256]{0,1:T(8,128)} async-done(((f32[1024,256]{0,1:T(8,128)}), f32[1024,256]{0,1:T(8,128)}) %all-reduce.12.cloned.1.call-update) | async-done | bytes 1048592 | tf_op jit(solution)/shard_map/psum | solution.py:20
  491.0 87.4 %all-reduce.20.cloned.1.call-done = (f32[4,1,256,256]{3,2,1,0:T(8,128)}, f32[4,1,256,256]{3,2,1,0:T(8,128)}) async-done(((f32[4,1,256,256]{3,2,1,0:T(8,128)}, f32[4,1,256,256]{3,2,1,0:T(8,128)}), (f32[4,1,256,256]{3,2,1,0:T(8,128)}, f32[4,1,256,256]{3,2,1,0:T(8,128)})) %all-reduce.20.cloned.1.call-update) | async-done | bytes 2097168 | tf_op jit(solution)/shard_map/psum | solution.py:20
  578.4 1.7 pad_maximum_fusion
  580.1 9.9 %convolution_subtract_fusion.1 = f32[1024,2048]{0,1:T(8,128)S(1)} fusion(f32[1024,2048]{0,1:T(8,128)} %copy-done.1, f32[1024,256]{0,1:T(8,128)S(1)} %copy-done.2, f32[2048,256]{1,0:T(8,128)S(1)} %bitcast.103), kind=kOutput, calls=%fused_computation.9 | convolution fusion | flops 6444548096 | bytes 19922944 | tf_op jit(solution)/shard_map/dot_general | solution.py:93
  590.0 3.4 copy-done
  594.7 83.6 %all-reduce.14.cloned.1.call-done = f32[256,256]{0,1:T(8,128)} async-done(((f32[256,256]{0,1:T(8,128)}), f32[256,256]{0,1:T(8,128)}) %all-reduce.14.cloned.1.call-update) | async-done | bytes 262160 | tf_op jit(solution)/shard_map/psum | solution.py:20
  680.4 11.7 %cholesky.164 = f32[128,128]{1,0:T(8,128)S(1)} custom-call(f32[128,128]{1,0:T(8,128)S(1)} %cholesky.197), custom_call_target="Cholesky" | custom-call | tf_op jit(solution)/shard_map/jit(cholesky)/cholesky | solution.py:81
  692.2 9.8 %custom-call.15 = f32[1,128,128]{1,2,0:T(8,128)S(1)} custom-call(f32[1,128,128]{2,1,0:T(8,128)S(1)} %get-tuple-element.57), custom_call_target="InvertDiagBlocksLowerTriangular" | custom-call | tf_op jit(solution)/shard_map/jit(cholesky)/cholesky | solution.py:81
  702.5 11.7 %cholesky.181 = f32[128,128]{1,0:T(8,128)S(1)} custom-call(f32[128,128]{1,0:T(8,128)S(1)} %convolution_subtract_fusion.4), custom_call_target="Cholesky" | custom-call | tf_op jit(solution)/shard_map/jit(cholesky)/cholesky | solution.py:81
  716.9 4.1 while.5
  721.1 19.7 %custom-call.16 = f32[2,128,128]{1,2,0:T(8,128)S(1)} custom-call(f32[2,128,128]{2,1,0:T(8,128)S(1)} %get-tuple-element.19), custom_call_target="InvertDiagBlocksLowerTriangular" | custom-call | tf_op jit(solution)/shard_map/triangular_solve/custom-call.0 | solution.py:82
  740.7 1.7 fusion.1
  745.8 59.7 %all-reduce.16.cloned.1.call-done = f32[1024,256]{0,1:T(8,128)} async-done(((f32[1024,256]{0,1:T(8,128)}), f32[1024,256]{0,1:T(8,128)}) %all-reduce.16.cloned.1.call-update) | async-done | bytes 1048592 | tf_op jit(solution)/shard_map/psum | solution.py:20
  805.5 2.5 broadcast_select_fusion.1
  808.1 2.5 copy.26
  813.5 2.9 copy.24
  816.4 85.7 %all-reduce.18.cloned.1.call-done = (f32[4,1,256,256]{3,2,1,0:T(8,128)}, f32[4,1,256,256]{3,2,1,0:T(8,128)}) async-done(((f32[4,1,256,256]{3,2,1,0:T(8,128)}, f32[4,1,256,256]{3,2,1,0:T(8,128)}), (f32[4,1,256,256]{3,2,1,0:T(8,128)}, f32[4,1,256,256]{3,2,1,0:T(8,128)})) %all-reduce.18.cloned.1.call-update) | async-done | bytes 2097168 | tf_op jit(solution)/shard_map/psum | solution.py:20
  903.7 11.0 %convolution_subtract_fusion = f32[1024,2048]{0,1:T(8,128)} fusion(f32[1024,2048]{0,1:T(8,128)} %copy-done, f32[1024,256]{0,1:T(8,128)S(1)} %copy-done.3, f32[2048,256]{1,0:T(8,128)S(1)} %bitcast.102), kind=kOutput, calls=%fused_computation.8 | convolution fusion | flops 6444548096 | bytes 19922944 | tf_op jit(solution)/shard_map/dot_general | solution.py:93
  914.7 10.5 %reshape.151 = f32[4,1,256,8,1,256]{2,0,5,3,4,1:T(4,128)} reshape(f32[1024,2048]{0,1:T(8,128)} %convolution_subtract_fusion) | data formatting | bytes 16777216 | tf_op jit(solution)/shard_map/reshape | solution.py:96
  925.3 20.5 %copy.19 = f32[4,1,256,8,1,256]{5,4,3,2,1,0:T(1,128)} copy(f32[4,1,256,8,1,256]{2,0,5,3,4,1:T(4,128)} %reshape.151) | data formatting | bytes 16777216
  (91 shorter events, 35.3 us)
Async XLA Ops:
  7.2 29.5 %all-gather.3.cloned.1.call-start = ((), (), s32[]{:S(2)}) async-start(), calls=%async_computation | async-start | bytes 1769472 | tf_op jit(solution)/shard_map/all_gather | solution.py:42
  7.9 185.5 %all-gather.5.cloned.1.call-start = ((), (), s32[]{:S(2)}) async-start(), calls=%async_computation.1 | async-start | bytes 26738688 | tf_op jit(solution)/shard_map/all_gather | solution.py:45
  36.6 159.3 %copy-start.4 = (bf16[4,1,256,768]{3,2,1,0:T(8,128)(2,1)S(1)}, bf16[4,1,256,768]{3,2,1,0:T(8,128)(2,1)}, u32[]{:S(2)}) copy-start(bf16[4,1,256,768]{3,2,1,0:T(8,128)(2,1)} %all-gather.3.cloned.1.call-done) | copy-start | bytes 4718596
  36.7 320.7 %all-reduce.10.cloned.1.call-start = ((), (), s32[]{:S(2)}) async-start(), calls=%async_computation.2 | async-start | bytes 524288 | tf_op jit(solution)/shard_map/psum | solution.py:20
  269.0 3.4 copy-start.1
  273.2 210.9 %all-reduce.12.cloned.1.call-start = ((), (), s32[]{:S(2)}) async-start(), calls=%async_computation.3 | async-start | bytes 2097152 | tf_op jit(solution)/shard_map/psum | solution.py:20
  422.5 155.9 %all-reduce.20.cloned.1.call-start = ((), (), s32[]{:S(2)}) async-start(), calls=%async_computation.7 | async-start | bytes 4194304 | tf_op jit(solution)/shard_map/psum | solution.py:20
  484.2 95.9 %copy-start.2 = (f32[1024,256]{0,1:T(8,128)S(1)}, f32[1024,256]{0,1:T(8,128)}, u32[]{:S(2)}) copy-start(f32[1024,256]{0,1:T(8,128)} %all-reduce.12.cloned.1.call-done) | copy-start | bytes 3145732
  488.4 189.9 %all-reduce.14.cloned.1.call-start = ((), (), s32[]{:S(2)}) async-start(), calls=%async_computation.4 | async-start | bytes 524288 | tf_op jit(solution)/shard_map/psum | solution.py:20
  590.0 3.4 copy-start
  594.2 211.3 %all-reduce.16.cloned.1.call-start = ((), (), s32[]{:S(2)}) async-start(), calls=%async_computation.5 | async-start | bytes 2097152 | tf_op jit(solution)/shard_map/psum | solution.py:20
  745.8 156.2 %all-reduce.18.cloned.1.call-start = ((), (), s32[]{:S(2)}) async-start(), calls=%async_computation.6 | async-start | bytes 4194304 | tf_op jit(solution)/shard_map/psum | solution.py:20
  805.5 6.4 copy-start.3
Sparse Core Ops, SparseCore 0:
  9.7 26.9 all-gather.2
  38.8 154.5 all-gather.4
  273.4 83.9 all-reduce.9
  422.6 61.4 all-reduce.11
  488.5 89.8 all-reduce.19
  594.4 83.8 all-reduce.13
  745.9 59.5 all-reduce.15
  812.1 89.8 all-reduce.17
where the time goes:
time: 963 us; the launch traced here: 953 us
  waiting for transfers between devices  642 us (67%)
  other arithmetic  127 us (13%)
  matrix products  103 us (11%)
  local copies, waits for them, and re-layouts  56.9 us (6%)
  between operations  22.5 us (2%)
    psum x6, waiting for transfers between devices, from_root(): return lax.psum(block, axis)  462 us
    all_gather x1, waiting for transfers between devices, per_device(): everything = lax.all_gather(row_inputs, 'row', axis=1, tiled=True)  151 us
    dot_general x1, matrix products, per_device(): jnp.dot(row_flat, column_flat.T, preferred_element_type=jnp.float32) / D0  73 us
    another operation x13, other arithmetic, per_device(): lower_factor = jnp.linalg.cholesky(pivot_block)  68.7 us
    another operation x5, other arithmetic, per_device(): lax.linalg.triangular_solve(lower_factor, panel_slab, left_side=False, lo...  39.4 us
    unnamed x16, local copies, waits for them, and re-layouts  30.2 us
    all_gather x1, waiting for transfers between devices, per_device(): row_inputs = lax.all_gather(inputs, 'col', axis=2, tiled=True)  28.7 us
    dot_general x2, matrix products, per_device(): jnp.dot(row_factor, column_factor.T, precision=lax.Precision.HIGHEST)  20.9 us
  transfers between devices with their start and end apart: 8, of which 8 were waited for; matrix products, arithmetic and copies ran while one was open for 1% of the time, Pallas kernels for 0%

commit v1 on v0

v1 whole, which is shorter than its diff:
```python
import math

import jax
import jax.numpy as jnp
from jax import lax
from jax.experimental import pallas as pl
from jax.experimental.pallas import tpu as pltpu
from jax.sharding import PartitionSpec as P

D0 = 768
TILE = 256
PANELS = 2
SPAN = PANELS * TILE
BLOCK = 128
PIVOTS = 8
BIAS = 0.1
RIDGE = 0.1
TINY = 1e-30
EXACT = lax.Precision.HIGHEST
F32 = jnp.float32
BF16 = jnp.bfloat16

ARC = (
    0.30011410855430565,
    0.014911524637152361,
    0.0027575196411184027,
    4.221988638112521e-06,
    0.0005224396428474578,
)


def matmul(left, right, left_dim, right_dim, precision=None):
    return lax.dot_general(
        left, right, (((left_dim,), (right_dim,)), ((), ())), precision=precision,
        preferred_element_type=F32,
    )


def split(value):
    high = value.astype(BF16)
    return high, (value - high.astype(F32)).astype(BF16)


def arc_term(gap):
    series = ARC[4] * gap + ARC[3]
    for coefficient in ARC[2::-1]:
        series = series * gap + coefficient
    return gap * gap * lax.rsqrt(gap) * series


def scales(squares):
    d0 = squares * (1.0 / D0)
    d1 = d0 + BIAS
    d2 = d1 + BIAS
    inverse1 = lax.rsqrt(d1)
    inverse2 = lax.rsqrt(d2)
    root_bias = math.sqrt(BIAS)
    return (
        lax.rsqrt(squares),
        root_bias * inverse1,
        jnp.sqrt(d0) * inverse1,
        root_bias * inverse2,
        jnp.sqrt(d1) * inverse2,
        jnp.sqrt(d2),
    )


def layers(product, rows, columns):
    cosine = product * rows[0] * columns[0]
    gap = jnp.maximum(1.0 - jnp.abs(cosine), TINY)
    value = jnp.maximum(cosine, 0.0) + arc_term(gap)
    for layer in (1, 3):
        gap = 1.0 - rows[layer] * columns[layer]
        gap = jnp.maximum(gap - rows[layer + 1] * columns[layer + 1] * value, TINY)
        value = (1.0 - gap) + arc_term(gap)
    return rows[5] * columns[5] * value


def row_squares(block):
    wide = block.astype(F32)
    return jnp.sum(wide * wide, axis=1, keepdims=True)


def column_squares(block):
    wide = block.astype(F32)
    high, low = split(wide * wide)
    ones = jnp.ones((16, D0), BF16)
    return (matmul(ones, high, 1, 1) + matmul(ones, low, 1, 1))[0:1]


def unit(shape):
    return lax.broadcasted_iota(jnp.int32, shape, 0) == lax.broadcasted_iota(jnp.int32, shape, 1)


def store_scales(squares, out):
    for index, vector in enumerate(scales(squares)):
        out[index] = jnp.broadcast_to(vector, out.shape[1:])


def factor_block(block):
    count = BLOCK // 8
    nb = PIVOTS
    lane = lax.broadcasted_iota(jnp.int32, (8, BLOCK), 1)
    sub = lax.broadcasted_iota(jnp.int32, (8, BLOCK), 0)
    block = list(block)
    inverse = [jnp.where(lane == sub + 8 * g, 1.0, 0.0).astype(F32) for g in range(count)]

    def spread(value):
        return jnp.broadcast_to(value, (8, BLOCK))

    for k in range(0, BLOCK, nb):
        g0, s = k // 8, k % 8
        groups = range(g0 + 1 if s + nb == 8 else g0, count)
        columns = [[None] * count for _ in range(nb)]
        for j in range(nb):
            for g in range(g0, count):
                columns[j][g] = spread(block[g][:, k + j:k + j + 1])
        left = [spread(block[g0][s + j:s + j + 1, :]) for j in range(nb)]
        right = [spread(inverse[g0][s + j:s + j + 1, :]) for j in range(nb)]
        pivot = {
            (i, j): spread(columns[j][g0][s + i:s + i + 1, :])
            for j in range(nb) for i in range(j, nb)
        }
        reciprocal = []
        lower = {}
        for j in range(nb):
            reciprocal.append(1.0 / pivot[j, j])
            for i in range(j + 1, nb):
                lower[i, j] = pivot[i, j] * reciprocal[j]
            for m in range(j + 1, nb):
                for i in range(m, nb):
                    pivot[i, m] = pivot[i, m] - lower[i, j] * pivot[m, j]
        for i in range(nb):
            for j in range(i):
                left[i] = left[i] - lower[i, j] * left[j]
                right[i] = right[i] - lower[i, j] * right[j]
        for g in groups:
            for i in range(nb):
                for j in range(i):
                    columns[i][g] = columns[i][g] - lower[i, j] * columns[j][g]
        left = [left[i] * reciprocal[i] for i in range(nb)]
        scaled = [right[i] * reciprocal[i] for i in range(nb)]
        for g in groups:
            one, two = block[g], inverse[g]
            for i in range(nb):
                if k + nb < BLOCK:
                    one = one - columns[i][g] * left[i]
                two = two - columns[i][g] * scaled[i]
            if g == g0:
                below = sub >= s + nb
                one = jnp.where(below, one, block[g])
                two = jnp.where(below, two, inverse[g])
            block[g], inverse[g] = one, two
        done = inverse[g0]
        for i in range(nb):
            done = jnp.where(sub == s + i, right[i] * lax.rsqrt(pivot[i, i]), done)
        inverse[g0] = done
    return inverse


def invert_factor(matrix, inverse):
    count = SPAN // BLOCK
    inverse[...] = jnp.zeros((SPAN, SPAN), F32)
    for index in range(count):
        o = index * BLOCK
        e = o + BLOCK
        slabs = [matrix[o + 8 * g:o + 8 * g + 8, o:e] for g in range(BLOCK // 8)]
        own = jnp.concatenate(factor_block(slabs), axis=0)
        if index > 0:
            inverse[o:e, 0:o] = matmul(own, inverse[o:e, 0:o], 1, 0, EXACT)
        inverse[o:e, o:e] = own
        if index < count - 1:
            upper = matmul(own, matrix[o:e, e:SPAN], 1, 0, EXACT)
            matrix[e:SPAN, e:SPAN] -= matmul(upper, upper, 0, 0, EXACT)
            inverse[e:SPAN, 0:e] -= matmul(upper, inverse[o:e, 0:e], 0, 0, EXACT)


def pivot_kernel(panel, high_out, low_out, mean_out, mean_row_out, center_out, center_row_out,
                 scales_out, scales_row_out, matrix, inverse):
    store_scales(row_squares(panel[...]), scales_out)
    for index, vector in enumerate(scales(column_squares(panel[...]))):
        scales_row_out[index] = vector
    for index in range(4):
        rows = slice(index * BLOCK, (index + 1) * BLOCK)
        product = matmul(panel[rows, :], panel[...], 1, 1)
        for lanes in range(4):
            columns = slice(lanes * BLOCK, (lanes + 1) * BLOCK)
            matrix[rows, columns] = BIAS + layers(
                product[:, columns],
                [scales_out[i, rows] for i in range(6)],
                [scales_row_out[i, :, columns] for i in range(6)],
            )
    mean_row = jnp.sum(matrix[...], axis=0, keepdims=True) * (1.0 / SPAN)
    mean_row_out[...] = mean_row
    mean = jnp.sum(matrix[...], axis=1, keepdims=True) * (1.0 / SPAN)
    mean_out[...] = jnp.broadcast_to(mean, mean_out.shape)
    matrix[...] += jnp.where(unit((SPAN, SPAN)), RIDGE, 0.0)
    invert_factor(matrix, inverse)
    high, low = split(inverse[...])
    high_out[...] = high
    low_out[...] = low
    center = jnp.sum(inverse[...] * mean_row, axis=1, keepdims=True)
    center_out[...] = jnp.broadcast_to(center, center_out.shape)
    center_row_out[...] = matmul(
        jnp.broadcast_to(mean_row, (8, SPAN)), inverse[...], 1, 1, EXACT
    )[0:1]


def main_kernel(place, row_inputs, column_inputs, panel, high_in, low_in, mean, mean_row, center,
                center_row, panel_scales, panel_scales_row, factor_out, trailing_out,
                column_high, column_low, column_scales, column_shift,
                row_scales, row_high, row_low, product, update):
    q = pl.program_id(0)
    row_position, column_position = place[0], place[1]

    def column_panel(p, _):
        block = column_inputs[p % 2, :, p // 2].reshape(TILE, D0)
        vectors = scales(column_squares(block))
        for index in range(6):
            column_scales[p, index] = vectors[index]
        product[...] = matmul(panel[...], block, 1, 1)

        def chunk(step, _):
            rows = pl.ds(pl.multiple_of(step * 64, 64), 64)
            for half in range(2):
                lanes = slice(half * 128, half * 128 + 128)
                product[rows, lanes] = (BIAS - mean[rows]) + layers(
                    product[rows, lanes],
                    [panel_scales[i, rows] for i in range(6)],
                    [vectors[i][:, lanes] for i in range(6)],
                )
            return 0

        lax.fori_loop(0, SPAN // 64, chunk, 0)
        for index in range(PANELS):
            @pl.when(place[2 + index] == p * 8 + column_position)
            def _():
                rows = slice(index * TILE, (index + 1) * TILE)
                product[rows, :] += jnp.where(unit((TILE, TILE)), RIDGE, 0.0)

        high, low = split(product[...])
        pieces = []
        for index in range(PANELS):
            rows = slice(index * TILE, (index + 1) * TILE)
            depth = (index + 1) * TILE
            pieces.append(
                matmul(high_in[rows, :depth], high[:depth], 1, 0)
                + (matmul(high_in[rows, :depth], low[:depth], 1, 0)
                   + matmul(low_in[rows, :depth], high[:depth], 1, 0))
            )
        factor = jnp.concatenate(pieces, axis=0)
        shift = 0.0
        for start in range(0, SPAN, 128):
            part = factor[start:start + 128]
            weight = center[start:start + 128]
            shift = shift + jnp.sum(
                part * jnp.concatenate([weight, weight], axis=1), axis=0, keepdims=True
            )
        column_shift[p] = shift
        high, low = split(factor)
        column_high[p] = high
        column_low[p] = low
        return 0

    @pl.when(q == 0)
    def _():
        lax.fori_loop(0, 8, column_panel, 0)

    own = row_inputs[:, 0].reshape(TILE, D0)
    store_scales(row_squares(own), row_scales)
    base = jnp.sum(center_row[...] * center_row[...], axis=1, keepdims=True)
    for index in range(PANELS):
        product[:TILE, :] = matmul(own, panel[index * TILE:(index + 1) * TILE, :], 1, 1)

        def chunk(step, _):
            rows = pl.ds(pl.multiple_of(step * 64, 64), 64)
            for half in range(2):
                lanes = slice(half * 128, half * 128 + 128)
                wide = slice(index * TILE + half * 128, index * TILE + half * 128 + 128)
                product[rows, lanes] = (BIAS - mean_row[:, wide]) + layers(
                    product[rows, lanes],
                    [row_scales[i, rows] for i in range(6)],
                    [panel_scales_row[i, :, wide] for i in range(6)],
                )
            return 0

        lax.fori_loop(0, TILE // 64, chunk, 0)

        @pl.when(place[2 + index] == q * 16 + row_position)
        def _():
            product[:TILE, :] += jnp.where(unit((TILE, TILE)), RIDGE, 0.0)

        high, low = split(product[:TILE, :])
        row_high[:, index * TILE:(index + 1) * TILE] = high
        row_low[:, index * TILE:(index + 1) * TILE] = low
    pieces = []
    for index in range(PANELS):
        rows = slice(index * TILE, (index + 1) * TILE)
        depth = (index + 1) * TILE
        high, low = row_high[:, :depth], row_low[:, :depth]
        pieces.append(
            matmul(high, high_in[rows, :depth], 1, 1)
            + (matmul(high, low_in[rows, :depth], 1, 1)
               + matmul(low, high_in[rows, :depth], 1, 1))
        )
    factor = jnp.concatenate(pieces, axis=1)
    factor_out[0] = factor + center_row[...]
    shift = (BIAS - base) - jnp.sum(factor * center_row[...], axis=1, keepdims=True)
    row_scales[6] = jnp.broadcast_to(shift, (TILE, 128))
    high, low = split(factor)
    row_high[...] = high
    row_low[...] = low

    def tile(p, _):
        block = column_inputs[p % 2, :, p // 2].reshape(TILE, D0)
        product[:TILE, :] = matmul(own, block, 1, 1)
        update[...] = matmul(row_high[...], column_high[p], 1, 0) + (
            matmul(row_high[...], column_low[p], 1, 0) + matmul(row_low[...], column_high[p], 1, 0)
        )

        @pl.when(q * 16 + row_position == p * 8 + column_position)
        def _():
            update[...] -= jnp.where(unit((TILE, TILE)), RIDGE, 0.0)

        def chunk(step, _):
            start = pl.multiple_of(step * 64, 64)
            rows = pl.ds(start, 64)
            for half in range(2):
                lanes = slice(half * 128, half * 128 + 128)
                value = layers(
                    product[rows, lanes],
                    [row_scales[i, rows] for i in range(6)],
                    [column_scales[p, i, :, lanes] for i in range(6)],
                )
                value = value + (row_scales[6, rows] - column_shift[p, :, lanes])
                value = value - update[rows, lanes]
                trailing_out[pl.ds(start * 16 + p * 2 + half, 64, stride=16), :] = value
            return 0

        lax.fori_loop(0, TILE // 64, chunk, 0)
        return 0

    lax.fori_loop(0, 8, tile, 0)


def whole(shape):
    return pl.BlockSpec(shape, lambda *_: (0,) * len(shape))


def call_pivot(panel):
    shapes = [
        ((SPAN, SPAN), BF16), ((SPAN, SPAN), BF16), ((SPAN, 128), F32), ((1, SPAN), F32),
        ((SPAN, 128), F32), ((1, SPAN), F32), ((6, SPAN, 128), F32), ((6, 1, SPAN), F32),
    ]
    return pl.pallas_call(
        pivot_kernel,
        out_shape=[jax.ShapeDtypeStruct(s, d) for s, d in shapes],
        scratch_shapes=[pltpu.VMEM((SPAN, SPAN), F32), pltpu.VMEM((SPAN, SPAN), F32)],
        compiler_params=pltpu.CompilerParams(vmem_limit_bytes=40 * 2**20),
        name="pivot",
    )(panel)


def call_main(place, row_inputs, column_inputs, panel, pivot):
    arrays = (panel, *pivot)
    return pl.pallas_call(
        main_kernel,
        grid=(4,),
        out_shape=[
            jax.ShapeDtypeStruct((4, TILE, SPAN), F32),
            jax.ShapeDtypeStruct((4 * TILE * 16, 128), F32),
        ],
        in_specs=[
            pl.BlockSpec(memory_space=pltpu.SMEM),
            pl.BlockSpec((8, 1, 32, D0), lambda q: (0, q, 0, 0)),
            whole((2, 8, 4, 32, D0)),
        ] + [whole(a.shape) for a in arrays],
        out_specs=[
            pl.BlockSpec((1, TILE, SPAN), lambda q: (q, 0, 0)),
            pl.BlockSpec((TILE * 16, 128), lambda q: (q, 0)),
        ],
        scratch_shapes=[
            pltpu.VMEM((8, SPAN, TILE), BF16),
            pltpu.VMEM((8, SPAN, TILE), BF16),
            pltpu.VMEM((8, 6, 1, TILE), F32),
            pltpu.VMEM((8, 1, TILE), F32),
            pltpu.VMEM((7, TILE, 128), F32),
            pltpu.VMEM((TILE, SPAN), BF16),
            pltpu.VMEM((TILE, SPAN), BF16),
            pltpu.VMEM((SPAN, TILE), F32),
            pltpu.VMEM((TILE, TILE), F32),
        ],
        compiler_params=pltpu.CompilerParams(vmem_limit_bytes=56 * 2**20),
        name="main",
    )(place, row_inputs, column_inputs, *arrays)


def exchange(block, axis, count):
    return lax.all_to_all(
        jnp.broadcast_to(block[None], (count,) + block.shape), axis, 0, 0, tiled=True
    )


def per_device(inputs, panel_order):
    own = inputs[:, 0]
    row_count = lax.axis_size("row")
    column_count = lax.axis_size("col")
    row_position = lax.axis_index("row")
    column_position = lax.axis_index("col")
    chosen = jnp.stack([
        lax.dynamic_index_in_dim(own, panel_order[k] // row_count, 0, keepdims=False)
        for k in range(PANELS)
    ])
    sent = chosen.reshape(PANELS, row_count, 2, D0).transpose(1, 0, 2, 3)
    came = lax.all_to_all(sent, "row", 0, 0, tiled=True)
    piece = jnp.stack([
        lax.dynamic_index_in_dim(came[:, k], panel_order[k] % row_count, 0, keepdims=False)
        for k in range(PANELS)
    ])
    gathered = exchange(piece, ("col", "row"), row_count * column_count)
    panel = gathered.transpose(1, 0, 2, 3).reshape(SPAN, D0)
    turn = [
        (r * column_count + c, (column_count * (r // column_count) + c) * column_count + r % column_count)
        for r in range(row_count) for c in range(column_count)
    ]
    row_inputs = exchange(own, "col", column_count)
    turned = lax.ppermute(own, ("row", "col"), turn)
    column_inputs = exchange(turned, "row", row_count).reshape(2, 8, 4, 32, D0)
    place = jnp.concatenate([
        jnp.stack([row_position, column_position]).astype(jnp.int32), panel_order
    ])
    pivot = call_pivot(panel)
    factor, trailing = call_main(place, row_inputs, column_inputs, panel, pivot)
    return factor.reshape(4, 1, TILE, SPAN), trailing.reshape(4, 1, TILE, 8, 1, TILE)


def solution(mesh):
    in_specs = (P(None, "row", "col", None), P())
    out_specs = (P(None, "row", None, None), P(None, "row", None, None, "col", None))
    return jax.shard_map(
        per_device, mesh=mesh, in_specs=in_specs, out_specs=out_specs, check_vma=False
    )
```

time: 963 us -> 211 us (0.22)
  waiting for transfers between devices: 642 us -> 42.5 us
  other arithmetic: 127 us -> 1.44 us
  matrix products: 103 us -> 0 us
  Pallas kernels: 0 us -> 98.8 us
  local copies, waits for them, and re-layouts: 56.9 us -> 13.1 us
  starting transfers between devices: 0.73 us -> 25.6 us
  blocking collectives: 0 us -> 22.5 us
  between operations: 22.5 us -> 6.01 us
    psum x6 -> x0, waiting for transfers between devices: 462 us -> none  [from_root(): return lax.psum(block, axis)]
    all_gather x2 -> x0, waiting for transfers between devices: 179 us -> none  [the longest x1 151 us: per_device(): everything = lax.all_gather(row_inputs, 'row', axis=1, tiled=True)]
    another operation x20 -> x1, other arithmetic: 111 us -> 0.01 us  [per_device(): jnp.stack([lax.dynamic_index_in_dim(came[:, k], panel_order[k] % row_coun...]
    pallas_call x0 -> x2, Pallas kernels: none -> 98.8 us  [the longest x1 73.9 us: call_main(): pl.pallas_call(main_kernel, grid=(4,), out_shape=[jax.ShapeDtypeStruct((4...]
    dot_general x3 -> x0, matrix products: 93.9 us -> none  [the longest x1 73 us: per_device(): jnp.dot(row_flat, column_flat.T, preferred_element_type=jnp.float32) / D0]
    all_to_all x0 -> x3, waiting for transfers between devices: none -> 42.5 us  [the longest x2 34.7 us: exchange(): lax.all_to_all(jnp.broadcast_to(block[None], (count,) + block.shape), axi...]
    all_to_all x0 -> x3, starting transfers between devices: none -> 24.9 us  [the longest x2 16.8 us: exchange(): lax.all_to_all(jnp.broadcast_to(block[None], (count,) + block.shape), axi...]
    unnamed x16 -> x24, local copies, waits for them, and re-layouts: 30.2 us -> 6.06 us
  transfers between devices with their start and end apart: 8 -> 4, of which waited for: 8 -> 3; matrix products, arithmetic and copies ran while one was open for 1% -> 1% of each run, Pallas kernels for 0% -> 12%
where the time goes in v1:
time: 211 us; the launch traced here: 210 us
  Pallas kernels  98.8 us (47%)
  waiting for transfers between devices  42.5 us (20%)
  starting transfers between devices  25.6 us (12%)
  blocking collectives  22.5 us (11%)
  local copies, waits for them, and re-layouts  13.1 us (6%)
  between operations  6.01 us (3%)
    pallas_call x1, Pallas kernels, call_main(): pl.pallas_call(main_kernel, grid=(4,), out_shape=[jax.ShapeDtypeStruct((4...  73.9 us
    all_to_all x2, waiting for transfers between devices, exchange(): lax.all_to_all(jnp.broadcast_to(block[None], (count,) + block.shape), axi...  34.7 us
    pallas_call x1, Pallas kernels, call_pivot(): pl.pallas_call(pivot_kernel, out_shape=[jax.ShapeDtypeStruct(s, d) for s,...  24.9 us
    all_to_all x1, blocking collectives, exchange(): lax.all_to_all(jnp.broadcast_to(block[None], (count,) + block.shape), axi...  22.5 us
    all_to_all x2, starting transfers between devices, exchange(): lax.all_to_all(jnp.broadcast_to(block[None], (count,) + block.shape), axi...  16.8 us
    all_to_all x1, starting transfers between devices, per_device(): came = lax.all_to_all(sent, 'row', 0, 0, tiled=True)  8.13 us
    all_to_all x1, waiting for transfers between devices, per_device(): came = lax.all_to_all(sent, 'row', 0, 0, tiled=True)  7.78 us
    unnamed x24, local copies, waits for them, and re-layouts  6.06 us
  transfers between devices with their start and end apart: 4, of which 3 were waited for; matrix products, arithmetic and copies ran while one was open for 1% of the time, Pallas kernels for 12%

profile of v1, /device:TPU:0, one launch (start us, length us, event | category | flops | bytes accessed | tf_op | source)
XLA Modules:
  0.0 209.9 jit_solution(16321649123421117825)
XLA Ops:
  0.6 0.0 copy-start.10
  0.6 1.3 fusion.1
  7.2 0.9 constant_dynamic-slice_fusion.1
  8.1 0.8 maximum_bitcast_fusion
  8.9 8.1 %all-to-all-start.2 = ((bf16[16,2,2,768]{3,2,1,0:T(2,128)(2,1)}), bf16[16,2,2,768]{3,2,1,0:T(2,128)(2,1)S(1)}, u32[]{:S(2)}, u32[]{:S(2)}) async-start(bf16[16,2,2,768]{3,2,1,0:T(2,128)(2,1)} %maximum_bitcast_fusion), calls=%async_computation.2 | async-start | bytes 196608 | tf_op jit(solution)/shard_map/all_to_all | solution.py:415
  17.1 7.8 %all-to-all-done.2 = bf16[16,2,2,768]{3,2,1,0:T(2,128)(2,1)S(1)} async-done(((bf16[16,2,2,768]{3,2,1,0:T(2,128)(2,1)}), bf16[16,2,2,768]{3,2,1,0:T(2,128)(2,1)S(1)}, u32[]{:S(2)}, u32[]{:S(2)}) %all-to-all-start.2) | async-done | bytes 98336 | tf_op jit(solution)/shard_map/all_to_all | solution.py:415
  24.8 0.1 fusion
  25.0 0.4 broadcast_in_dim.22
  25.4 22.5 %all_to_all.20 = bf16[128,2,2,768]{3,2,1,0:T(2,128)(2,1)S(1)} all-to-all(bf16[128,2,2,768]{3,2,1,0:T(2,128)(2,1)S(1)} %broadcast_in_dim.22), channel_id=1, replica_groups=mesh['row'=16,'col'=8] {'col','row'}, dimensions={0} | all-to-all | bytes 1572864 | tf_op jit(solution)/shard_map/all_to_all | solution.py:399
  47.8 0.0 copy-done.10
  47.8 1.3 broadcast_in_dim.9
  49.2 3.6 %all-to-all-start = ((bf16[8,4,32,768]{3,2,1,0:T(8,128)(2,1)}), bf16[8,4,32,768]{3,2,1,0:T(8,128)(2,1)S(1)}, u32[]{:S(2)}, u32[]{:S(2)}) async-start(bf16[8,4,32,768]{3,2,1,0:T(8,128)(2,1)} %broadcast_in_dim.9), calls=%async_computation | async-start | bytes 3145728 | tf_op jit(solution)/shard_map/all_to_all | solution.py:399
  52.8 0.7 collective-permute-start
  53.4 0.0 collective-permute-done
  53.4 21.4 %all-to-all-done.row_inputs = bf16[8,4,32,768]{3,2,1,0:T(8,128)(2,1)S(1)} async-done(((bf16[8,4,32,768]{3,2,1,0:T(8,128)(2,1)}), bf16[8,4,32,768]{3,2,1,0:T(8,128)(2,1)S(1)}, u32[]{:S(2)}, u32[]{:S(2)}) %all-to-all-start) | async-done | bytes 1572896 | tf_op jit(solution)/shard_map/all_to_all | solution.py:399
  74.8 2.2 %broadcast_in_dim.10 = bf16[16,4,32,768]{3,2,1,0:T(8,128)(2,1)} broadcast(bf16[4,32,768]{2,1,0:T(8,128)(2,1)S(1)} %collective-permute-done), dimensions={1,2,3} | broadcast | bytes 3342336 | tf_op jit(solution)/shard_map/broadcast_in_dim | solution.py:400
  77.0 13.2 %all-to-all-start.1 = ((bf16[16,4,32,768]{3,2,1,0:T(8,128)(2,1)}), bf16[16,4,32,768]{3,2,1,0:T(8,128)(2,1)}, u32[]{:S(2)}, u32[]{:S(2)}) async-start(bf16[16,4,32,768]{3,2,1,0:T(8,128)(2,1)} %broadcast_in_dim.10), calls=%async_computation.1 | async-start | bytes 6291456 | tf_op jit(solution)/shard_map/all_to_all | solution.py:399
  90.2 0.7 pad_add_fusion.place
  90.9 0.5 copy.6
  91.4 0.3 reshape.29.panel
  91.7 0.0 copy-start
  91.7 24.9 %pivot.1 = (bf16[512,512]{1,0:T(8,128)(2,1)S(1)}, bf16[512,512]{1,0:T(8,128)(2,1)S(1)}, f32[512,128]{1,0:T(8,128)S(1)}, f32[1,512]{1,0:T(1,128)S(1)}, f32[512,12...) custom-call(bf16[512,768]{1,0:T(8,128)(2,1)S(1)} %reshape.29.panel), custom_call_target="tpu_custom_call" | custom-call | tf_op jit(solution)/shard_map/pivot/pallas_call | solution.py:355
  116.7 1.2 copy-done.1
  117.9 0.8 copy-done.2
  118.7 0.8 copy-done.3
  119.5 0.7 copy-done.4
  120.2 0.7 copy-done.5
  120.9 0.6 copy-done.6
  121.5 0.6 copy-done.7
  122.1 0.6 copy-done.8
  122.7 13.4 %all-to-all-done.1 = bf16[16,4,32,768]{3,2,1,0:T(8,128)(2,1)} async-done(((bf16[16,4,32,768]{3,2,1,0:T(8,128)(2,1)}), bf16[16,4,32,768]{3,2,1,0:T(8,128)(2,1)}, u32[]{:S(2)}, u32[]{:S(2)}) %all-to-all-start.1) | async-done | bytes 3145760 | tf_op jit(solution)/shard_map/all_to_all | solution.py:399
  136.1 73.9 %main.1 = (f32[4,256,512]{2,1,0:T(8,128)}, f32[16384,128]{1,0:T(8,128)}) custom-call(s32[4]{0:T(128)} %pad_add_fusion.place, bf16[8,4,32,768]{3,2,1,0:T(8,128)(2,1)} %copy-done.9, bf16[2,8,4,32,768]{4,3,2,1,0:T(8,128)(2,1)} %bitcast.3.column_inputs, bf16[512,768]{1,0:T(8,128)(2,1)} %copy-done, bf16[512,512]{1,0:T(8,128)(2,1)} %copy-done.2, ...), custom_call_target="tpu_custom_call" | custom-call | tf_op jit(solution)/shard_map/main/pallas_call | solution.py:366
  (17 shorter events, 0.1 us)
Async XLA Ops:
  0.6 47.2 %copy-start.10 = (bf16[4,1,32,768]{3,2,1,0:T(8,128)(2,1)S(1)}, bf16[4,1,32,768]{3,2,1,0:T(8,128)(2,1)}, u32[]{:S(2)}) copy-start(bf16[4,1,32,768]{3,2,1,0:T(8,128)(2,1)} %param.2) | copy-start | bytes 589828
  8.9 16.0 %all-to-all-start.2 = ((bf16[16,2,2,768]{3,2,1,0:T(2,128)(2,1)}), bf16[16,2,2,768]{3,2,1,0:T(2,128)(2,1)S(1)}, u32[]{:S(2)}, u32[]{:S(2)}) async-start(bf16[16,2,2,768]{3,2,1,0:T(2,128)(2,1)} %maximum_bitcast_fusion), calls=%async_computation.2 | async-start | bytes 196608 | tf_op jit(solution)/shard_map/all_to_all | solution.py:415
  49.2 25.7 %all-to-all-start = ((bf16[8,4,32,768]{3,2,1,0:T(8,128)(2,1)}), bf16[8,4,32,768]{3,2,1,0:T(8,128)(2,1)S(1)}, u32[]{:S(2)}, u32[]{:S(2)}) async-start(bf16[8,4,32,768]{3,2,1,0:T(8,128)(2,1)} %broadcast_in_dim.9), calls=%async_computation | async-start | bytes 3145728 | tf_op jit(solution)/shard_map/all_to_all | solution.py:399
  52.8 0.7 collective-permute-start
  74.8 2.2 %copy-start.9 = (bf16[8,4,32,768]{3,2,1,0:T(8,128)(2,1)}, bf16[8,4,32,768]{3,2,1,0:T(8,128)(2,1)S(1)}, u32[]{:S(2)}) copy-start(bf16[8,4,32,768]{3,2,1,0:T(8,128)(2,1)S(1)} %all-to-all-done.row_inputs) | copy-start | bytes 4718596
  77.0 13.2 %copy-start.11 = (s32[2]{0:T(128)S(1)}, s32[2]{0:T(128)}, u32[]{:S(2)}) copy-start(s32[2]{0:T(128)} %param.3) | copy-start | bytes 28
  77.0 59.0 %all-to-all-start.1 = ((bf16[16,4,32,768]{3,2,1,0:T(8,128)(2,1)}), bf16[16,4,32,768]{3,2,1,0:T(8,128)(2,1)}, u32[]{:S(2)}, u32[]{:S(2)}) async-start(bf16[16,4,32,768]{3,2,1,0:T(8,128)(2,1)} %broadcast_in_dim.10), calls=%async_computation.1 | async-start | bytes 6291456 | tf_op jit(solution)/shard_map/all_to_all | solution.py:399
  91.7 44.3 %copy-start = (bf16[512,768]{1,0:T(8,128)(2,1)}, bf16[512,768]{1,0:T(8,128)(2,1)S(1)}, u32[]{:S(2)}) copy-start(bf16[512,768]{1,0:T(8,128)(2,1)S(1)} %reshape.29.panel) | copy-start | bytes 2359300
  116.7 1.2 copy-start.1
  117.9 0.8 copy-start.2
  118.7 0.9 copy-start.3
  119.5 0.7 copy-start.4
  120.2 0.7 copy-start.5
  120.9 0.6 copy-start.6
  121.5 0.6 copy-start.7
  122.1 0.6 copy-start.8

commit v2 on v1

v2 whole, which is shorter than its diff:
```python
import math

import jax
import jax.numpy as jnp
from jax import lax
from jax.experimental import pallas as pl
from jax.experimental.pallas import tpu as pltpu
from jax.sharding import PartitionSpec as P

D0 = 768
TILE = 256
PANELS = 2
SPAN = PANELS * TILE
BLOCK = 128
PIVOTS = 8
BIAS = 0.1
RIDGE = 0.1
TINY = 1e-30
EXACT = lax.Precision.HIGHEST
F32 = jnp.float32
BF16 = jnp.bfloat16

ARC = (
    0.30011410855430565,
    0.014911524637152361,
    0.0027575196411184027,
    4.221988638112521e-06,
    0.0005224396428474578,
)


def matmul(left, right, left_dim, right_dim, precision=None):
    return lax.dot_general(
        left, right, (((left_dim,), (right_dim,)), ((), ())), precision=precision,
        preferred_element_type=F32,
    )


def split(value):
    high = value.astype(BF16)
    return high, (value - high.astype(F32)).astype(BF16)


def arc_term(gap):
    series = ARC[4] * gap + ARC[3]
    for coefficient in ARC[2::-1]:
        series = series * gap + coefficient
    return gap * gap * lax.rsqrt(gap) * series


def scales(squares):
    d0 = squares * (1.0 / D0)
    d1 = d0 + BIAS
    d2 = d1 + BIAS
    inverse1 = lax.rsqrt(d1)
    inverse2 = lax.rsqrt(d2)
    root_bias = math.sqrt(BIAS)
    return (
        lax.rsqrt(squares),
        root_bias * inverse1,
        jnp.sqrt(d0) * inverse1,
        root_bias * inverse2,
        jnp.sqrt(d1) * inverse2,
        jnp.sqrt(d2),
    )


def layers(product, rows, columns):
    cosine = product * rows[0] * columns[0]
    gap = jnp.maximum(1.0 - jnp.abs(cosine), TINY)
    value = jnp.maximum(cosine, 0.0) + arc_term(gap)
    for layer in (1, 3):
        gap = 1.0 - rows[layer] * columns[layer]
        gap = jnp.maximum(gap - rows[layer + 1] * columns[layer + 1] * value, TINY)
        value = (1.0 - gap) + arc_term(gap)
    return rows[5] * columns[5] * value


def row_squares(block):
    wide = block.astype(F32)
    return jnp.sum(wide * wide, axis=1, keepdims=True)


def column_squares(block):
    wide = block.astype(F32)
    high, low = split(wide * wide)
    ones = jnp.ones((16, D0), BF16)
    return (matmul(ones, high, 1, 1) + matmul(ones, low, 1, 1))[0:1]


def unit(shape):
    return lax.broadcasted_iota(jnp.int32, shape, 0) == lax.broadcasted_iota(jnp.int32, shape, 1)


def store_scales(squares, out):
    for index, vector in enumerate(scales(squares)):
        out[index] = jnp.broadcast_to(vector, out.shape[1:])


def factor_block(block):
    count = BLOCK // 8
    nb = PIVOTS
    lane = lax.broadcasted_iota(jnp.int32, (8, BLOCK), 1)
    sub = lax.broadcasted_iota(jnp.int32, (8, BLOCK), 0)
    block = list(block)
    inverse = [jnp.where(lane == sub + 8 * g, 1.0, 0.0).astype(F32) for g in range(count)]

    def spread(value):
        return jnp.broadcast_to(value, (8, BLOCK))

    for k in range(0, BLOCK, nb):
        g0, s = k // 8, k % 8
        groups = range(g0 + 1 if s + nb == 8 else g0, count)
        columns = [[None] * count for _ in range(nb)]
        for j in range(nb):
            for g in range(g0, count):
                columns[j][g] = spread(block[g][:, k + j:k + j + 1])
        left = [spread(block[g0][s + j:s + j + 1, :]) for j in range(nb)]
        right = [spread(inverse[g0][s + j:s + j + 1, :]) for j in range(nb)]
        pivot = {
            (i, j): spread(columns[j][g0][s + i:s + i + 1, :])
            for j in range(nb) for i in range(j, nb)
        }
        reciprocal = []
        lower = {}
        for j in range(nb):
            reciprocal.append(1.0 / pivot[j, j])
            for i in range(j + 1, nb):
                lower[i, j] = pivot[i, j] * reciprocal[j]
            for m in range(j + 1, nb):
                for i in range(m, nb):
                    pivot[i, m] = pivot[i, m] - lower[i, j] * pivot[m, j]
        for i in range(nb):
            for j in range(i):
                left[i] = left[i] - lower[i, j] * left[j]
                right[i] = right[i] - lower[i, j] * right[j]
        for g in groups:
            for i in range(nb):
                for j in range(i):
                    columns[i][g] = columns[i][g] - lower[i, j] * columns[j][g]
        left = [left[i] * reciprocal[i] for i in range(nb)]
        scaled = [right[i] * reciprocal[i] for i in range(nb)]
        for g in groups:
            one, two = block[g], inverse[g]
            for i in range(nb):
                if k + nb < BLOCK:
                    one = one - columns[i][g] * left[i]
                two = two - columns[i][g] * scaled[i]
            if g == g0:
                below = sub >= s + nb
                one = jnp.where(below, one, block[g])
                two = jnp.where(below, two, inverse[g])
            block[g], inverse[g] = one, two
        done = inverse[g0]
        for i in range(nb):
            done = jnp.where(sub == s + i, right[i] * lax.rsqrt(pivot[i, i]), done)
        inverse[g0] = done
    return inverse


def invert_factor(matrix, inverse):
    count = SPAN // BLOCK
    inverse[...] = jnp.zeros((SPAN, SPAN), F32)
    for index in range(count):
        o = index * BLOCK
        e = o + BLOCK
        slabs = [matrix[o + 8 * g:o + 8 * g + 8, o:e] for g in range(BLOCK // 8)]
        own = jnp.concatenate(factor_block(slabs), axis=0)
        if index > 0:
            inverse[o:e, 0:o] = matmul(own, inverse[o:e, 0:o], 1, 0, EXACT)
        inverse[o:e, o:e] = own
        if index < count - 1:
            upper = matmul(own, matrix[o:e, e:SPAN], 1, 0, EXACT)
            matrix[e:SPAN, e:SPAN] -= matmul(upper, upper, 0, 0, EXACT)
            inverse[e:SPAN, 0:e] -= matmul(upper, inverse[o:e, 0:e], 0, 0, EXACT)


def choose_kernel(order, own, out):
    for k in range(PANELS):
        rows = own[order[k] // 16].astype(F32)
        for device in range(16):
            start = device % 4 * 8
            out[device, k] = rows[start:start + 8].astype(BF16)


def pick_kernel(order, came, out):
    for k in range(PANELS):
        rows = came[order[k] % 16, k]
        for device in range(16):
            out[device, k] = rows


def pivot_kernel(mine, other, panel, high_out, low_out, mean_out, mean_row_out, center_out, center_row_out,
                 scales_out, scales_row_out, matrix, inverse):
    core = lax.axis_index("col") % 2
    for source, side in ((mine, core), (other, 1 - core)):
        for k in range(PANELS):
            for x in range(4):
                for y in (0, 2):
                    rows = [source[(y + i) * 4 + x, k].astype(F32) for i in range(2)]
                    start = pl.multiple_of(k * TILE + 64 * x + 32 * side + 8 * y, 16)
                    panel[pl.ds(start, 16), :] = jnp.concatenate(rows, axis=0).astype(BF16)
    store_scales(row_squares(panel[...]), scales_out)
    for index, vector in enumerate(scales(column_squares(panel[...]))):
        scales_row_out[index] = vector
    for index in range(4):
        rows = slice(index * BLOCK, (index + 1) * BLOCK)
        product = matmul(panel[rows, :], panel[...], 1, 1)
        for lanes in range(4):
            columns = slice(lanes * BLOCK, (lanes + 1) * BLOCK)
            matrix[rows, columns] = BIAS + layers(
                product[:, columns],
                [scales_out[i, rows] for i in range(6)],
                [scales_row_out[i, :, columns] for i in range(6)],
            )
    mean_row = jnp.sum(matrix[...], axis=0, keepdims=True) * (1.0 / SPAN)
    mean_row_out[...] = mean_row
    mean = jnp.sum(matrix[...], axis=1, keepdims=True) * (1.0 / SPAN)
    mean_out[...] = jnp.broadcast_to(mean, mean_out.shape)
    matrix[...] += jnp.where(unit((SPAN, SPAN)), RIDGE, 0.0)
    invert_factor(matrix, inverse)
    high, low = split(inverse[...])
    high_out[...] = high
    low_out[...] = low
    center = jnp.sum(inverse[...] * mean_row, axis=1, keepdims=True)
    center_out[...] = jnp.broadcast_to(center, center_out.shape)
    center_row_out[...] = matmul(
        jnp.broadcast_to(mean_row, (8, SPAN)), inverse[...], 1, 1, EXACT
    )[0:1]


def eye_term(start, lanes, amount):
    row = lax.broadcasted_iota(jnp.int32, (64, 128), 0) + (start - lanes)
    return jnp.where(row == lax.broadcasted_iota(jnp.int32, (64, 128), 1), amount, 0.0)


def main_kernel(order, row_inputs, column_inputs, panel,
                high_in, low_in, mean, mean_row, center, center_row, panel_scales,
                panel_scales_row, factor_out, trailing_out,
                column_high, column_low, column_scales, column_shift,
                own, row_scales, row_high, row_low, row_factor,
                product0, product1, update0, update1, high0, high1, low0, low1):
    group = pl.program_id(0)
    row_position, column_position = lax.axis_index("row"), lax.axis_index("col")
    product, update = (product0, product1), (update0, update1)
    panel_high, panel_low = (high0, high1), (low0, low1)

    def column_block(p):
        return column_inputs[p % 2, :, p // 2].reshape(TILE, D0)

    def ridge_of(tile, index):
        return jnp.where(order[index] == tile, RIDGE, 0.0).astype(F32)

    def column_first(p, slot):
        block = column_block(p)
        product[slot][...] = matmul(panel[...], block, 1, 1)
        for index, vector in enumerate(scales(column_squares(block))):
            column_scales[p, index] = vector

    def column_middle(p, slot):
        for start in range(0, SPAN, 64):
            index = start // TILE
            ridge = ridge_of(p * 8 + column_position, index)
            rows = slice(start, start + 64)
            for lanes in (0, 128):
                wide = slice(lanes, lanes + 128)
                value = (BIAS - mean[rows]) + layers(
                    product[slot][rows, wide],
                    [panel_scales[i, rows] for i in range(6)],
                    [column_scales[p, i, :, wide] for i in range(6)],
                )
                if start % TILE // 128 * 128 == lanes:
                    value = value + eye_term(start % TILE, lanes, ridge)
                high, low = split(value)
                panel_high[slot][rows, wide] = high
                panel_low[slot][rows, wide] = low

    def column_last(p, slot):
        shift = 0.0
        for index in range(PANELS):
            rows = slice(index * TILE, (index + 1) * TILE)
            depth = (index + 1) * TILE
            high, low = panel_high[slot][:depth, :], panel_low[slot][:depth, :]
            factor = matmul(high_in[rows, :depth], high, 1, 0) + (
                matmul(high_in[rows, :depth], low, 1, 0) + matmul(low_in[rows, :depth], high, 1, 0)
            )
            weight = center[rows]
            shift = shift + jnp.sum(
                factor * jnp.concatenate([weight, weight], axis=1), axis=0, keepdims=True
            )
            high, low = split(factor)
            column_high[p, rows] = high
            column_low[p, rows] = low
        column_shift[p] = shift

    def row_first(q, slot):
        block = own[pl.ds(pl.multiple_of(q * TILE, TILE), TILE), :]
        for index in range(PANELS):
            rows = slice(index * TILE, (index + 1) * TILE)
            product[slot][rows, :] = matmul(block, panel[rows, :], 1, 1)

    def row_middle(q, slot):
        for index in range(PANELS):
            ridge = ridge_of(q * 16 + row_position, index)
            for start in range(0, TILE, 64):
                rows = pl.ds(pl.multiple_of(q * TILE + start, 64), 64)
                here = slice(index * TILE + start, index * TILE + start + 64)
                for lanes in (0, 128):
                    wide = slice(index * TILE + lanes, index * TILE + lanes + 128)
                    value = (BIAS - mean_row[:, wide]) + layers(
                        product[slot][here, lanes:lanes + 128],
                        [row_scales[i, rows] for i in range(6)],
                        [panel_scales_row[i, :, wide] for i in range(6)],
                    )
                    if start // 128 * 128 == lanes:
                        value = value + eye_term(start, lanes, ridge)
                    high, low = split(value)
                    panel_high[slot][here, lanes:lanes + 128] = high
                    panel_low[slot][here, lanes:lanes + 128] = low

    def row_last(q, slot):
        rows = pl.ds(pl.multiple_of(q * TILE, TILE), TILE)
        shift = BIAS - jnp.sum(center_row[...] * center_row[...], axis=1, keepdims=True)
        for index in range(PANELS):
            wide = slice(index * TILE, (index + 1) * TILE)
            factor = 0.0
            for part in range(index + 1):
                depth = slice(part * TILE, (part + 1) * TILE)
                high, low = panel_high[slot][depth, :], panel_low[slot][depth, :]
                factor = factor + (
                    matmul(high, high_in[wide, depth], 1, 1)
                    + (matmul(high, low_in[wide, depth], 1, 1) + matmul(low, high_in[wide, depth], 1, 1))
                )
            row_factor[rows, wide] = factor + center_row[:, wide]
            shift = shift - jnp.sum(factor * center_row[:, wide], axis=1, keepdims=True)
            high, low = split(factor)
            row_high[rows, wide] = high
            row_low[rows, wide] = low
        row_scales[6, rows] = jnp.broadcast_to(shift, (TILE, 128))

    def pipeline(count, first, middle, last):
        first(0, 0)

        def pair(step, _):
            for slot in range(2):
                at = step * 2 + slot
                last(jnp.maximum(at - 1, 0), 1 - slot)
                first(jnp.minimum(at + 1, count - 1), 1 - slot)
                middle(at, slot)
            return 0

        lax.fori_loop(0, count // 2, pair, 0)
        last(count - 1, 1)

    @pl.when(group == 0)
    def _():
        for q in range(4):
            own[q * TILE:(q + 1) * TILE, :] = row_inputs[:, q].reshape(TILE, D0)
        for start in range(0, 4 * TILE, 128):
            for index, vector in enumerate(scales(row_squares(own[start:start + 128, :]))):
                row_scales[index, start:start + 128] = jnp.broadcast_to(vector, (128, 128))
        pipeline(4, row_first, row_middle, row_last)
        pipeline(8, column_first, column_middle, column_last)

    for half in range(2):
        rows = pl.ds(pl.multiple_of(group * 2 * TILE + half * TILE, TILE), TILE)
        factor_out[half] = row_factor[rows, :]

    def tile_first(p, slot):
        rows = slice(slot * SPAN, (slot + 1) * SPAN)
        product[slot][...] = matmul(own[rows, :], column_block(p), 1, 1)
        update[slot][...] = matmul(row_high[rows, :], column_high[p], 1, 0) + (
            matmul(row_high[rows, :], column_low[p], 1, 0)
            + matmul(row_low[rows, :], column_high[p], 1, 0)
        )

    def tile_middle(p, slot):
        for start in range(0, SPAN, 64):
            here = slice(start, start + 64)
            rows = slice(slot * SPAN + start, slot * SPAN + start + 64)
            for half in range(2):
                wide = slice(half * 128, half * 128 + 128)
                value = layers(
                    product[slot][here, wide],
                    [row_scales[i, rows] for i in range(6)],
                    [column_scales[p, i, :, wide] for i in range(6)],
                )
                value = value + (row_scales[6, rows] - column_shift[p, :, wide])
                value = value - update[slot][here, wide]
                trailing_out[rows, p % 4 * 2 + half, :] = value

    tile_first(group * 4, 0)

    def tile(step, _):
        p = group * 4 + step
        tile_first(p, 1)
        tile_middle(p, 0)
        tile_first(jnp.minimum(p + 1, 7), 0)
        tile_middle(p, 1)
        return 0

    lax.fori_loop(0, 4, tile, 0)

    @pl.when(row_position % 8 == column_position)
    def _():
        for part in range(2):
            q = group * 2 + part
            p = part * 2 + row_position // 8
            for start in range(0, TILE, 64):
                half = start // 128
                at = pl.ds(pl.multiple_of(q * TILE + start, 64), 64)
                trailing_out[at, p * 2 + half, :] += eye_term(start, half * 128, RIDGE)


def whole(shape):
    return pl.BlockSpec(shape, lambda *_: (0,) * len(shape))


def call_small(kernel, order, block, name):
    return pl.pallas_call(
        kernel,
        out_shape=jax.ShapeDtypeStruct((16, PANELS, 8, D0), BF16),
        in_specs=[pl.BlockSpec(memory_space=pltpu.SMEM), pl.BlockSpec(memory_space=pltpu.VMEM)],
        name=name,
    )(order, block)


def call_pivot(mine, other):
    shapes = [
        ((SPAN, D0), BF16),
        ((SPAN, SPAN), BF16), ((SPAN, SPAN), BF16), ((SPAN, 128), F32), ((1, SPAN), F32),
        ((SPAN, 128), F32), ((1, SPAN), F32), ((6, SPAN, 128), F32), ((6, 1, SPAN), F32),
    ]
    return pl.pallas_call(
        pivot_kernel,
        out_shape=[jax.ShapeDtypeStruct(s, d) for s, d in shapes],
        in_specs=[pl.BlockSpec(memory_space=pltpu.VMEM)] * 2,
        scratch_shapes=[pltpu.VMEM((SPAN, SPAN), F32), pltpu.VMEM((SPAN, SPAN), F32)],
        compiler_params=pltpu.CompilerParams(vmem_limit_bytes=60 * 2**20),
        cost_estimate=pl.CostEstimate(flops=3 * 10**10, bytes_accessed=4 * 10**6, transcendentals=0),
        name="pivot",
    )(mine, other)


def call_main(order, row_inputs, column_inputs, arrays):
    factor, trailing = pl.pallas_call(
        main_kernel,
        grid=(2,),
        out_shape=[
            jax.ShapeDtypeStruct((4, TILE, SPAN), F32),
            jax.ShapeDtypeStruct((4 * TILE, 16, 128), F32),
        ],
        in_specs=[pl.BlockSpec(memory_space=pltpu.SMEM)]
        + [pl.BlockSpec(memory_space=pltpu.VMEM)] * (2 + len(arrays)),
        out_specs=[
            pl.BlockSpec((2, TILE, SPAN), lambda g: (g, 0, 0)),
            pl.BlockSpec((4 * TILE, 8, 128), lambda g: (0, g, 0)),
        ],
        scratch_shapes=[
            pltpu.VMEM((8, SPAN, TILE), BF16),
            pltpu.VMEM((8, SPAN, TILE), BF16),
            pltpu.VMEM((8, 6, 1, TILE), F32),
            pltpu.VMEM((8, 1, TILE), F32),
            pltpu.VMEM((4 * TILE, D0), BF16),
            pltpu.VMEM((7, 4 * TILE, 128), F32),
            pltpu.VMEM((4 * TILE, SPAN), BF16),
            pltpu.VMEM((4 * TILE, SPAN), BF16),
            pltpu.VMEM((4 * TILE, SPAN), F32),
        ] + [pltpu.VMEM((SPAN, TILE), F32)] * 4 + [pltpu.VMEM((SPAN, TILE), BF16)] * 4,
        compiler_params=pltpu.CompilerParams(vmem_limit_bytes=60 * 2**20),
        name="main",
    )(order, row_inputs, column_inputs, *arrays)
    return factor, trailing


def exchange(block, axes, groups):
    return lax.all_to_all(block, axes, 0, 0, tiled=True, axis_index_groups=groups)


def per_device(inputs, panel_order):
    own = inputs[:, 0]
    row_count = lax.axis_size("row")
    column_count = lax.axis_size("col")
    turn = [
        (r * column_count + c, (column_count * (r // column_count) + c) * column_count + r % column_count)
        for r in range(row_count) for c in range(column_count)
    ]
    turned = lax.ppermute(own, ("row", "col"), turn)
    row_inputs = lax.all_gather(own, "col", axis=0)
    swap = [(c, c ^ 1) for c in range(column_count)]
    sent = call_small(choose_kernel, panel_order, own, "choose")
    came = exchange(sent, "row", None)
    came, turned = lax.optimization_barrier((came, turned))
    column_inputs = lax.all_gather(turned, "row", axis=0).reshape(2, 8, 4, 32, D0)
    piece = call_small(pick_kernel, panel_order, came, "pick")
    groups = [
        [(z * 4 + y) * column_count + 2 * x + core for y in range(4) for x in range(4)]
        for z in range(row_count // 4) for core in range(2)
    ]
    mine = exchange(piece, ("row", "col"), groups)
    other = lax.ppermute(mine, "col", swap)
    pivot = call_pivot(mine, other)
    factor, trailing = call_main(panel_order, row_inputs, column_inputs, pivot)
    return factor.reshape(4, 1, TILE, SPAN), trailing.reshape(4, 1, TILE, 8, 1, TILE)


def solution(mesh):
    in_specs = (P(None, "row", "col", None), P())
    out_specs = (P(None, "row", None, None), P(None, "row", None, None, "col", None))
    return jax.shard_map(
        per_device, mesh=mesh, in_specs=in_specs, out_specs=out_specs, check_vma=False
    )
```

time: 211 us -> 160 us (0.76)
  waiting for transfers between devices: 42.5 us -> 16.3 us
  starting transfers between devices: 25.6 us -> 9.8 us
  local copies, waits for them, and re-layouts: 13.1 us -> 1.47 us
  between operations: 6.01 us -> 14.1 us
  Pallas kernels: 98.8 us -> 90.8 us
  blocking collectives: 22.5 us -> 27.3 us
    all_to_all x3 -> x1, waiting for transfers between devices: 42.5 us -> 8.44 us  [exchange(): lax.all_to_all(block, axes, 0, 0, tiled=True, axis_index_groups=groups)]
    all_to_all x3 -> x1, starting transfers between devices: 24.9 us -> 8.13 us  [exchange(): lax.all_to_all(block, axes, 0, 0, tiled=True, axis_index_groups=groups)]
    pallas_call x1 -> x3, Pallas kernels: 73.9 us -> 64.2 us  [the longest x1 60.7 us: call_main(): pl.pallas_call(main_kernel, grid=(2,), out_shape=[jax.ShapeDtypeStruct((4...]
    all_gather x0 -> x2, waiting for transfers between devices: none -> 5.48 us  [the longest x1 5.48 us: per_device(): lax.all_gather(turned, 'row', axis=0).reshape(2, 8, 4, 32, D0)]
    all_to_all x1, blocking collectives: 22.5 us -> 27.3 us  [exchange(): lax.all_to_all(block, axes, 0, 0, tiled=True, axis_index_groups=groups)]
    unnamed x24 -> x8, local copies, waits for them, and re-layouts: 6.06 us -> 1.47 us
    broadcast_in_dim x3 -> x0, local copies, waits for them, and re-layouts: 3.91 us -> none  [exchange(): jnp.broadcast_to(block[None], (count,) + block.shape)]
  transfers between devices with their start and end apart: 4 -> 5, of which waited for: 3 -> 3; matrix products, arithmetic and copies ran while one was open for 1% -> 0% of each run, Pallas kernels for 12% -> 19%
where the time goes in v2:
time: 160 us
  Pallas kernels  90.8 us (57%)
  blocking collectives  27.3 us (17%)
  waiting for transfers between devices  16.3 us (10%)
  between operations  14.1 us (9%)
  starting transfers between devices  9.8 us (6%)
    pallas_call x1, Pallas kernels, call_main(): pl.pallas_call(main_kernel, grid=(2,), out_shape=[jax.ShapeDtypeStruct((4...  60.7 us
    all_to_all x1, blocking collectives, exchange(): lax.all_to_all(block, axes, 0, 0, tiled=True, axis_index_groups=groups)  27.3 us
    pallas_call x1, Pallas kernels, call_pivot(): pl.pallas_call(pivot_kernel, out_shape=[jax.ShapeDtypeStruct(s, d) for s,...  26.6 us
    all_to_all x1, waiting for transfers between devices, exchange(): lax.all_to_all(block, axes, 0, 0, tiled=True, axis_index_groups=groups)  8.44 us
    all_to_all x1, starting transfers between devices, exchange(): lax.all_to_all(block, axes, 0, 0, tiled=True, axis_index_groups=groups)  8.13 us
    all_gather x1, waiting for transfers between devices, per_device(): lax.all_gather(turned, 'row', axis=0).reshape(2, 8, 4, 32, D0)  5.48 us
    pallas_call x2, Pallas kernels, call_small(): pl.pallas_call(kernel, out_shape=jax.ShapeDtypeStruct((16, PANELS, 8, D0)...  3.51 us
  transfers between devices with their start and end apart: 5, of which 3 were waited for; matrix products, arithmetic and copies ran while one was open for 0% of the time, Pallas kernels for 19%

profile of v2, /device:TPU:0, one launch (start us, length us, event | category | flops | bytes accessed | tf_op | source)
XLA Modules:
  0.0 159.8 jit_solution(7529629629494748732)
XLA Ops:
  7.2 0.0 all-gather.5.cloned.1.call-start
  7.2 0.7 all-gather.5.cloned.1.call-update
  7.9 1.7 %choose.1 = bf16[16,2,8,768]{3,2,1,0:T(8,128)(2,1)} custom-call(s32[2]{0:T(128)} %order.5, bf16[4,32,768]{2,1,0:T(8,128)(2,1)} %bitcast.9), custom_call_target="tpu_custom_call" | custom-call | tf_op jit(solution)/shard_map/choose/pallas_call | solution.py:420
  9.6 8.1 %all-to-all-start = ((bf16[16,2,8,768]{3,2,1,0:T(8,128)(2,1)}), bf16[16,2,8,768]{3,2,1,0:T(8,128)(2,1)S(1)}, u32[]{:S(2)}, u32[]{:S(2)}) async-start(bf16[16,2,8,768]{3,2,1,0:T(8,128)(2,1)} %choose.1), calls=%async_computation | async-start | bytes 786432 | tf_op jit(solution)/shard_map/all_to_all | solution.py:477
  17.8 0.0 all-gather.7.cloned.1.call-start
  17.8 1.6 collective-permute-start
  19.4 0.0 collective-permute-done
  19.4 0.0 copy-start.2
  19.4 8.4 %all-to-all-done.came = bf16[16,2,8,768]{3,2,1,0:T(8,128)(2,1)S(1)} async-done(((bf16[16,2,8,768]{3,2,1,0:T(8,128)(2,1)}), bf16[16,2,8,768]{3,2,1,0:T(8,128)(2,1)S(1)}, u32[]{:S(2)}, u32[]{:S(2)}) %all-to-all-start) | async-done | bytes 393248 | tf_op jit(solution)/shard_map/all_to_all | solution.py:477
  27.8 0.0 copy-start
  27.8 0.0 copy-done.2
  27.8 0.0 all-gather.7.cloned.1.call-update
  27.9 0.7 copy-done
  28.6 1.8 %pick.1 = bf16[16,2,8,768]{3,2,1,0:T(8,128)(2,1)} custom-call(s32[2]{0:T(128)} %order.5, bf16[16,2,8,768]{3,2,1,0:T(8,128)(2,1)} %copy-done), custom_call_target="tpu_custom_call" | custom-call | tf_op jit(solution)/shard_map/pick/pallas_call | solution.py:420
  30.4 27.3 %all_to_all.10.mine = bf16[16,2,8,768]{3,2,1,0:T(8,128)(2,1)S(1)} all-to-all(bf16[16,2,8,768]{3,2,1,0:T(8,128)(2,1)} %pick.1), channel_id=1, replica_groups={{0,2,4,6,8,10,12,14,16,18,20,22,24,26,28,30},{1,3,5,7,9,11,13,15,17,19,..., dimensions={0} | all-to-all | bytes 786432 | tf_op jit(solution)/shard_map/all_to_all | solution.py:477
  57.7 0.0 copy-start.1
  57.7 0.0 collective-permute-start.1
  57.7 1.7 %collective-permute-done.1.other = bf16[16,2,8,768]{3,2,1,0:T(8,128)(2,1)S(1)} collective-permute-done((bf16[16,2,8,768]{3,2,1,0:T(8,128)(2,1)S(1)}, bf16[16,2,8,768]{3,2,1,0:T(8,128)(2,1)S(1)}, u32[]{:S(2)}, u32[]{:S(2)}) %collective-permute-start.1) | collective-permute-done | bytes 393248 | tf_op jit(solution)/shard_map/ppermute | solution.py:501
  59.4 0.0 copy-done.1
  59.4 0.0 copy-start.3
  59.4 0.7 copy-done.3
  60.1 26.6 %pivot.1 = (bf16[512,768]{1,0:T(8,128)(2,1)}, bf16[512,512]{1,0:T(8,128)(2,1)}, bf16[512,512]{1,0:T(8,128)(2,1)}, f32[512,128]{1,0:T(8,128)}, f32[1,512]{1,0:T(1...) custom-call(bf16[16,2,8,768]{3,2,1,0:T(8,128)(2,1)} %copy-done.1, ...), custom_call_target="tpu_custom_call" | custom-call | flops 30000001024 | bytes 4000000 | tf_op jit(solution)/shard_map/pivot/pallas_call | solution.py:434
  86.8 0.0 all-gather.5.cloned.1.call-done
  86.8 5.5 %all-gather.7.cloned.1.call-done = bf16[64,32,768]{2,1,0:T(8,128)(2,1)} async-done(((bf16[4,32,768]{2,1,0:T(8,128)(2,1)}), bf16[64,32,768]{2,1,0:T(8,128)(2,1)}) %all-gather.7.cloned.1.call-update) | async-done | bytes 3145744 | tf_op jit(solution)/shard_map/all_gather | solution.py:494
  92.2 60.7 %main.1 = (f32[4,256,512]{2,1,0:T(8,128)}, f32[1024,16,128]{2,1,0:T(8,128)}) custom-call(s32[2]{0:T(128)} %order.5, bf16[8,4,32,768]{3,2,1,0:T(8,128)(2,1)} %bitcast.8, bf16[2,8,4,32,768]{4,3,2,1,0:T(8,128)(2,1)} %bitcast.7, bf16[512,768]{1,0:T(8,128)(2,1)} %get-tuple-element.17.panel, bf16[512,512]{1,0:T(8,128)(2,1)} %get-tuple-element.18.high_in, ...), custom_call_target="tpu_custom_call" | custom-call | tf_op jit(solution)/shard_map/main/pallas_call | solution.py:446
Async XLA Ops:
  7.2 79.6 %all-gather.5.cloned.1.call-start = ((), (), s32[]{:S(2)}) async-start(), calls=%async_computation.2 | async-start | bytes 1769472 | tf_op jit(solution)/shard_map/all_gather | solution.py:489
  9.6 18.2 %all-to-all-start = ((bf16[16,2,8,768]{3,2,1,0:T(8,128)(2,1)}), bf16[16,2,8,768]{3,2,1,0:T(8,128)(2,1)S(1)}, u32[]{:S(2)}, u32[]{:S(2)}) async-start(bf16[16,2,8,768]{3,2,1,0:T(8,128)(2,1)} %choose.1), calls=%async_computation | async-start | bytes 786432 | tf_op jit(solution)/shard_map/all_to_all | solution.py:477
  17.8 74.5 %all-gather.7.cloned.1.call-start = ((), (), s32[]{:S(2)}) async-start(), calls=%async_computation.3 | async-start | bytes 3342336 | tf_op jit(solution)/shard_map/all_gather | solution.py:494
  17.8 1.6 collective-permute-start
  19.4 8.5 %copy-start.2 = (bf16[4,32,768]{2,1,0:T(8,128)(2,1)}, bf16[4,32,768]{2,1,0:T(8,128)(2,1)S(1)}, u32[]{:S(2)}) copy-start(bf16[4,32,768]{2,1,0:T(8,128)(2,1)S(1)} %collective-permute-done) | copy-start | bytes 589828
  27.8 0.7 copy-start
  57.7 1.7 %copy-start.1 = (bf16[16,2,8,768]{3,2,1,0:T(8,128)(2,1)}, bf16[16,2,8,768]{3,2,1,0:T(8,128)(2,1)S(1)}, u32[]{:S(2)}) copy-start(bf16[16,2,8,768]{3,2,1,0:T(8,128)(2,1)S(1)} %all_to_all.10.mine) | copy-start | bytes 1179652
  57.7 1.7 %collective-permute-start.1 = (bf16[16,2,8,768]{3,2,1,0:T(8,128)(2,1)S(1)}, bf16[16,2,8,768]{3,2,1,0:T(8,128)(2,1)S(1)}, u32[]{:S(2)}, u32[]{:S(2)}) collective-permute-start(bf16[16,2,8,768]{3,2,1,0:T(8,128)(2,1)S(1)} %all_to_all.10.mine), channel_id=1, source_target_pairs={{0,1},{1,0},{2,3},{3,2},{4,5},{5,4},{6,7},{7,6},{8,9},{9,8},{10,11... | collective-permute-start | bytes 1179656 | tf_op jit(solution)/shard_map/ppermute | solution.py:501
  59.4 0.7 copy-start.3
Sparse Core Ops, SparseCore 0:
  9.7 32.0 all-gather.4
  43.9 48.2 all-gather.6

commit v3 on v2

--- a/solution.py
+++ b/solution.py
@@ -82,10 +82,7 @@
 
 
 def column_squares(block):
-    wide = block.astype(F32)
-    high, low = split(wide * wide)
-    ones = jnp.ones((16, D0), BF16)
-    return (matmul(ones, high, 1, 1) + matmul(ones, low, 1, 1))[0:1]
+    return jnp.transpose(jnp.broadcast_to(row_squares(block), (block.shape[0], 128)))[0:1]
 
 
 def unit(shape):
@@ -387,8 +384,10 @@
                 )
                 value = value + (row_scales[6, rows] - column_shift[p, :, wide])
                 value = value - update[slot][here, wide]
-                trailing_out[rows, p % 4 * 2 + half, :] = value
-
+                at = (slot * SPAN + start) * 8 + p % 4 * 2 + half
+                trailing[pl.ds(at, 64, stride=8), :] = value
+
+    trailing = trailing_out.reshape(4 * TILE * 8, 128)
     tile_first(group * 4, 0)
 
     def tile(step, _):

time: 160 us -> 154 us (0.963)
  Pallas kernels: 90.8 us -> 83.8 us
    pallas_call x1, Pallas kernels: 60.7 us -> 54.1 us  [call_main(): pl.pallas_call(main_kernel, grid=(2,), out_shape=[jax.ShapeDtypeStruct((4...]
where the time goes in v3:
time: 154 us; the launch traced here: 153 us
  Pallas kernels  83.8 us (54%)
  blocking collectives  27.3 us (18%)
  waiting for transfers between devices  16.8 us (11%)
  between operations  14.1 us (9%)
  starting transfers between devices  9.8 us (6%)
    pallas_call x1, Pallas kernels, call_main(): pl.pallas_call(main_kernel, grid=(2,), out_shape=[jax.ShapeDtypeStruct((4...  54.1 us
    all_to_all x1, blocking collectives, exchange(): lax.all_to_all(block, axes, 0, 0, tiled=True, axis_index_groups=groups)  27.3 us
    pallas_call x1, Pallas kernels, call_pivot(): pl.pallas_call(pivot_kernel, out_shape=[jax.ShapeDtypeStruct(s, d) for s,...  26.2 us
    all_to_all x1, waiting for transfers between devices, exchange(): lax.all_to_all(block, axes, 0, 0, tiled=True, axis_index_groups=groups)  8.44 us
    all_to_all x1, starting transfers between devices, exchange(): lax.all_to_all(block, axes, 0, 0, tiled=True, axis_index_groups=groups)  8.13 us
    all_gather x1, waiting for transfers between devices, per_device(): lax.all_gather(turned, 'row', axis=0).reshape(2, 8, 4, 32, D0)  5.92 us
    pallas_call x2, Pallas kernels, call_small(): pl.pallas_call(kernel, out_shape=jax.ShapeDtypeStruct((16, PANELS, 8, D0)...  3.51 us
  transfers between devices with their start and end apart: 5, of which 3 were waited for; matrix products, arithmetic and copies ran while one was open for 0% of the time, Pallas kernels for 19%

profile of v3, /device:TPU:0, one launch (start us, length us, event | category | flops | bytes accessed | tf_op | source)
XLA Modules:
  0.0 153.1 jit_solution(8178694515928251720)
XLA Ops:
  7.2 0.0 all-gather.5.cloned.1.call-start
  7.2 0.7 all-gather.5.cloned.1.call-update
  7.9 1.7 %choose.1 = bf16[16,2,8,768]{3,2,1,0:T(8,128)(2,1)} custom-call(s32[2]{0:T(128)} %order.5, bf16[4,32,768]{2,1,0:T(8,128)(2,1)} %bitcast.9), custom_call_target="tpu_custom_call" | custom-call | tf_op jit(solution)/shard_map/choose/pallas_call | solution.py:419
  9.6 8.1 %all-to-all-start = ((bf16[16,2,8,768]{3,2,1,0:T(8,128)(2,1)}), bf16[16,2,8,768]{3,2,1,0:T(8,128)(2,1)S(1)}, u32[]{:S(2)}, u32[]{:S(2)}) async-start(bf16[16,2,8,768]{3,2,1,0:T(8,128)(2,1)} %choose.1), calls=%async_computation | async-start | bytes 786432 | tf_op jit(solution)/shard_map/all_to_all | solution.py:476
  17.8 0.0 all-gather.7.cloned.1.call-start
  17.8 1.6 %collective-permute-start = (bf16[4,32,768]{2,1,0:T(8,128)(2,1)}, bf16[4,32,768]{2,1,0:T(8,128)(2,1)S(1)}, u32[]{:S(2)}, u32[]{:S(2)}) collective-permute-start(bf16[4,32,768]{2,1,0:T(8,128)(2,1)} %bitcast.10), channel_id=1, source_target_pairs={{0,0},{1,8},{2,16},{3,24},{4,32},{5,40},{6,48},{7,56},{8,1},{9,9},... | collective-permute-start | bytes 589832 | tf_op jit(solution)/shard_map/ppermute | solution.py:487
  19.4 0.0 collective-permute-done
  19.4 0.0 copy-start.2
  19.4 8.4 %all-to-all-done.came = bf16[16,2,8,768]{3,2,1,0:T(8,128)(2,1)S(1)} async-done(((bf16[16,2,8,768]{3,2,1,0:T(8,128)(2,1)}), bf16[16,2,8,768]{3,2,1,0:T(8,128)(2,1)S(1)}, u32[]{:S(2)}, u32[]{:S(2)}) %all-to-all-start) | async-done | bytes 393248 | tf_op jit(solution)/shard_map/all_to_all | solution.py:476
  27.8 0.0 copy-start
  27.8 0.0 copy-done.2
  27.8 0.0 all-gather.7.cloned.1.call-update
  27.9 0.7 copy-done
  28.6 1.8 %pick.1 = bf16[16,2,8,768]{3,2,1,0:T(8,128)(2,1)} custom-call(s32[2]{0:T(128)} %order.5, bf16[16,2,8,768]{3,2,1,0:T(8,128)(2,1)} %copy-done), custom_call_target="tpu_custom_call" | custom-call | tf_op jit(solution)/shard_map/pick/pallas_call | solution.py:419
  30.4 27.3 %all_to_all.10.mine = bf16[16,2,8,768]{3,2,1,0:T(8,128)(2,1)S(1)} all-to-all(bf16[16,2,8,768]{3,2,1,0:T(8,128)(2,1)} %pick.1), channel_id=1, replica_groups={{0,2,4,6,8,10,12,14,16,18,20,22,24,26,28,30},{1,3,5,7,9,11,13,15,17,19,..., dimensions={0} | all-to-all | bytes 786432 | tf_op jit(solution)/shard_map/all_to_all | solution.py:476
  57.7 0.0 copy-start.1
  57.7 0.0 collective-permute-start.1
  57.7 1.7 %collective-permute-done.1.other = bf16[16,2,8,768]{3,2,1,0:T(8,128)(2,1)S(1)} collective-permute-done((bf16[16,2,8,768]{3,2,1,0:T(8,128)(2,1)S(1)}, bf16[16,2,8,768]{3,2,1,0:T(8,128)(2,1)S(1)}, u32[]{:S(2)}, u32[]{:S(2)}) %collective-permute-start.1) | collective-permute-done | bytes 393248 | tf_op jit(solution)/shard_map/ppermute | solution.py:500
  59.4 0.0 copy-done.1
  59.4 0.0 copy-start.3
  59.4 0.7 copy-done.3
  60.1 26.2 %pivot.1 = (bf16[512,768]{1,0:T(8,128)(2,1)}, bf16[512,512]{1,0:T(8,128)(2,1)}, bf16[512,512]{1,0:T(8,128)(2,1)}, f32[512,128]{1,0:T(8,128)}, f32[1,512]{1,0:T(1...) custom-call(bf16[16,2,8,768]{3,2,1,0:T(8,128)(2,1)} %copy-done.1, ...), custom_call_target="tpu_custom_call" | custom-call | flops 30000001024 | bytes 4000000 | tf_op jit(solution)/shard_map/pivot/pallas_call | solution.py:433
  86.3 0.0 all-gather.5.cloned.1.call-done
  86.3 5.9 %all-gather.7.cloned.1.call-done = bf16[64,32,768]{2,1,0:T(8,128)(2,1)} async-done(((bf16[4,32,768]{2,1,0:T(8,128)(2,1)}), bf16[64,32,768]{2,1,0:T(8,128)(2,1)}) %all-gather.7.cloned.1.call-update) | async-done | bytes 3145744 | tf_op jit(solution)/shard_map/all_gather | solution.py:493
  92.2 54.1 %main.1 = (f32[4,256,512]{2,1,0:T(8,128)}, f32[1024,16,128]{2,1,0:T(8,128)}) custom-call(s32[2]{0:T(128)} %order.5, bf16[8,4,32,768]{3,2,1,0:T(8,128)(2,1)} %bitcast.8, bf16[2,8,4,32,768]{4,3,2,1,0:T(8,128)(2,1)} %bitcast.7, bf16[512,768]{1,0:T(8,128)(2,1)} %get-tuple-element.17.panel, bf16[512,512]{1,0:T(8,128)(2,1)} %get-tuple-element.18.high_in, ...), custom_call_target="tpu_custom_call" | custom-call | tf_op jit(solution)/shard_map/main/pallas_call | solution.py:445
Async XLA Ops:
  7.2 79.1 %all-gather.5.cloned.1.call-start = ((), (), s32[]{:S(2)}) async-start(), calls=%async_computation.2 | async-start | bytes 1769472 | tf_op jit(solution)/shard_map/all_gather | solution.py:488
  9.6 18.2 %all-to-all-start = ((bf16[16,2,8,768]{3,2,1,0:T(8,128)(2,1)}), bf16[16,2,8,768]{3,2,1,0:T(8,128)(2,1)S(1)}, u32[]{:S(2)}, u32[]{:S(2)}) async-start(bf16[16,2,8,768]{3,2,1,0:T(8,128)(2,1)} %choose.1), calls=%async_computation | async-start | bytes 786432 | tf_op jit(solution)/shard_map/all_to_all | solution.py:476
  17.8 74.5 %all-gather.7.cloned.1.call-start = ((), (), s32[]{:S(2)}) async-start(), calls=%async_computation.3 | async-start | bytes 3342336 | tf_op jit(solution)/shard_map/all_gather | solution.py:493
  17.8 1.6 %collective-permute-start = (bf16[4,32,768]{2,1,0:T(8,128)(2,1)}, bf16[4,32,768]{2,1,0:T(8,128)(2,1)S(1)}, u32[]{:S(2)}, u32[]{:S(2)}) collective-permute-start(bf16[4,32,768]{2,1,0:T(8,128)(2,1)} %bitcast.10), channel_id=1, source_target_pairs={{0,0},{1,8},{2,16},{3,24},{4,32},{5,40},{6,48},{7,56},{8,1},{9,9},... | collective-permute-start | bytes 589832 | tf_op jit(solution)/shard_map/ppermute | solution.py:487
  19.4 8.5 %copy-start.2 = (bf16[4,32,768]{2,1,0:T(8,128)(2,1)}, bf16[4,32,768]{2,1,0:T(8,128)(2,1)S(1)}, u32[]{:S(2)}) copy-start(bf16[4,32,768]{2,1,0:T(8,128)(2,1)S(1)} %collective-permute-done) | copy-start | bytes 589828
  27.8 0.7 copy-start
  57.7 1.7 %copy-start.1 = (bf16[16,2,8,768]{3,2,1,0:T(8,128)(2,1)}, bf16[16,2,8,768]{3,2,1,0:T(8,128)(2,1)S(1)}, u32[]{:S(2)}) copy-start(bf16[16,2,8,768]{3,2,1,0:T(8,128)(2,1)S(1)} %all_to_all.10.mine) | copy-start | bytes 1179652
  57.7 1.7 %collective-permute-start.1 = (bf16[16,2,8,768]{3,2,1,0:T(8,128)(2,1)S(1)}, bf16[16,2,8,768]{3,2,1,0:T(8,128)(2,1)S(1)}, u32[]{:S(2)}, u32[]{:S(2)}) collective-permute-start(bf16[16,2,8,768]{3,2,1,0:T(8,128)(2,1)S(1)} %all_to_all.10.mine), channel_id=1, source_target_pairs={{0,1},{1,0},{2,3},{3,2},{4,5},{5,4},{6,7},{7,6},{8,9},{9,8},{10,11... | collective-permute-start | bytes 1179656 | tf_op jit(solution)/shard_map/ppermute | solution.py:500
  59.4 0.7 copy-start.3
Sparse Core Ops, SparseCore 0:
  9.7 32.0 all-gather.4
  43.9 48.2 all-gather.6

commit v4 on v3

--- a/solution.py
+++ b/solution.py
@@ -466,7 +466,7 @@
             pltpu.VMEM((4 * TILE, SPAN), BF16),
             pltpu.VMEM((4 * TILE, SPAN), F32),
         ] + [pltpu.VMEM((SPAN, TILE), F32)] * 4 + [pltpu.VMEM((SPAN, TILE), BF16)] * 4,
-        compiler_params=pltpu.CompilerParams(vmem_limit_bytes=60 * 2**20),
+        compiler_params=pltpu.CompilerParams(vmem_limit_bytes=46 * 2**20),
         name="main",
     )(order, row_inputs, column_inputs, *arrays)
     return factor, trailing

time: 154 us -> 162 us (1.052)
  local copies, waits for them, and re-layouts: 1.47 us -> 11.5 us
  Pallas kernels: 83.8 us -> 82.1 us
    unnamed x8 -> x30, local copies, waits for them, and re-layouts: 1.47 us -> 11.5 us
    pallas_call x1, Pallas kernels: 54.1 us -> 52.4 us  [call_main(): pl.pallas_call(main_kernel, grid=(2,), out_shape=[jax.ShapeDtypeStruct((4...]
  transfers between devices with their start and end apart: 5 -> 5, of which waited for: 3 -> 3; matrix products, arithmetic and copies ran while one was open for 0% -> 0% of each run, Pallas kernels for 19% -> 18%
where the time goes in v4:
time: 162 us
  Pallas kernels  82.1 us (51%)
  blocking collectives  27.3 us (17%)
  waiting for transfers between devices  16.8 us (10%)
  between operations  14.1 us (9%)
  local copies, waits for them, and re-layouts  11.5 us (7%)
  starting transfers between devices  9.8 us (6%)
    pallas_call x1, Pallas kernels, call_main(): pl.pallas_call(main_kernel, grid=(2,), out_shape=[jax.ShapeDtypeStruct((4...  52.4 us
    all_to_all x1, blocking collectives, exchange(): lax.all_to_all(block, axes, 0, 0, tiled=True, axis_index_groups=groups)  27.3 us
    pallas_call x1, Pallas kernels, call_pivot(): pl.pallas_call(pivot_kernel, out_shape=[jax.ShapeDtypeStruct(s, d) for s,...  26.2 us
    unnamed x30, local copies, waits for them, and re-layouts  11.5 us
    all_to_all x1, waiting for transfers between devices, exchange(): lax.all_to_all(block, axes, 0, 0, tiled=True, axis_index_groups=groups)  8.44 us
    all_to_all x1, starting transfers between devices, exchange(): lax.all_to_all(block, axes, 0, 0, tiled=True, axis_index_groups=groups)  8.13 us
    all_gather x1, waiting for transfers between devices, per_device(): lax.all_gather(turned, 'row', axis=0).reshape(2, 8, 4, 32, D0)  5.92 us
    pallas_call x2, Pallas kernels, call_small(): pl.pallas_call(kernel, out_shape=jax.ShapeDtypeStruct((16, PANELS, 8, D0)...  3.51 us
  transfers between devices with their start and end apart: 5, of which 3 were waited for; matrix products, arithmetic and copies ran while one was open for 0% of the time, Pallas kernels for 18%

profile of v4, /device:TPU:0, one launch (start us, length us, event | category | flops | bytes accessed | tf_op | source)
XLA Modules:
  0.0 161.5 jit_solution(10358955731828862060)
XLA Ops:
  7.2 0.0 all-gather.5.cloned.1.call-start
  7.2 0.7 all-gather.5.cloned.1.call-update
  7.9 1.7 %choose.1 = bf16[16,2,8,768]{3,2,1,0:T(8,128)(2,1)} custom-call(s32[2]{0:T(128)} %order.5, bf16[4,32,768]{2,1,0:T(8,128)(2,1)} %bitcast.9), custom_call_target="tpu_custom_call" | custom-call | tf_op jit(solution)/shard_map/choose/pallas_call | solution.py:419
  9.6 8.1 %all-to-all-start = ((bf16[16,2,8,768]{3,2,1,0:T(8,128)(2,1)}), bf16[16,2,8,768]{3,2,1,0:T(8,128)(2,1)S(1)}, u32[]{:S(2)}, u32[]{:S(2)}) async-start(bf16[16,2,8,768]{3,2,1,0:T(8,128)(2,1)} %choose.1), calls=%async_computation | async-start | bytes 786432 | tf_op jit(solution)/shard_map/all_to_all | solution.py:476
  17.8 0.0 all-gather.7.cloned.1.call-start
  17.8 1.6 collective-permute-start
  19.4 0.0 collective-permute-done
  19.4 0.0 copy-start.13
  19.4 8.4 %all-to-all-done.came = bf16[16,2,8,768]{3,2,1,0:T(8,128)(2,1)S(1)} async-done(((bf16[16,2,8,768]{3,2,1,0:T(8,128)(2,1)}), bf16[16,2,8,768]{3,2,1,0:T(8,128)(2,1)S(1)}, u32[]{:S(2)}, u32[]{:S(2)}) %all-to-all-start) | async-done | bytes 393248 | tf_op jit(solution)/shard_map/all_to_all | solution.py:476
  27.8 0.0 copy-done.13
  27.8 0.0 all-gather.7.cloned.1.call-update
  27.9 0.7 copy-done.11
  28.6 1.8 %pick.1 = bf16[16,2,8,768]{3,2,1,0:T(8,128)(2,1)} custom-call(s32[2]{0:T(128)} %order.5, bf16[16,2,8,768]{3,2,1,0:T(8,128)(2,1)} %copy-done.11), custom_call_target="tpu_custom_call" | custom-call | tf_op jit(solution)/shard_map/pick/pallas_call | solution.py:419
  30.4 27.3 %all_to_all.10.mine = bf16[16,2,8,768]{3,2,1,0:T(8,128)(2,1)S(1)} all-to-all(bf16[16,2,8,768]{3,2,1,0:T(8,128)(2,1)} %pick.1), channel_id=1, replica_groups={{0,2,4,6,8,10,12,14,16,18,20,22,24,26,28,30},{1,3,5,7,9,11,13,15,17,19,..., dimensions={0} | all-to-all | bytes 786432 | tf_op jit(solution)/shard_map/all_to_all | solution.py:476
  57.7 0.0 collective-permute-start.1
  57.7 1.7 %collective-permute-done.1.other = bf16[16,2,8,768]{3,2,1,0:T(8,128)(2,1)S(1)} collective-permute-done((bf16[16,2,8,768]{3,2,1,0:T(8,128)(2,1)S(1)}, bf16[16,2,8,768]{3,2,1,0:T(8,128)(2,1)S(1)}, u32[]{:S(2)}, u32[]{:S(2)}) %collective-permute-start.1) | collective-permute-done | bytes 393248 | tf_op jit(solution)/shard_map/ppermute | solution.py:500
  59.4 0.0 copy-done.12
  59.4 0.8 copy-done.14
  60.2 26.2 %pivot.1 = (bf16[512,768]{1,0:T(8,128)(2,1)}, bf16[512,512]{1,0:T(8,128)(2,1)}, bf16[512,512]{1,0:T(8,128)(2,1)}, f32[512,128]{1,0:T(8,128)}, f32[1,512]{1,0:T(1...) custom-call(bf16[16,2,8,768]{3,2,1,0:T(8,128)(2,1)} %copy-done.12, ...), custom_call_target="tpu_custom_call" | custom-call | flops 30000001024 | bytes 4000000 | tf_op jit(solution)/shard_map/pivot/pallas_call | solution.py:433
  86.3 5.9 %all-gather.7.cloned.1.call-done = bf16[64,32,768]{2,1,0:T(8,128)(2,1)} async-done(((bf16[4,32,768]{2,1,0:T(8,128)(2,1)}), bf16[64,32,768]{2,1,0:T(8,128)(2,1)}) %all-gather.7.cloned.1.call-update) | async-done | bytes 3145744 | tf_op jit(solution)/shard_map/all_gather | solution.py:493
  92.2 0.0 copy-done.8
  92.2 1.4 copy-done
  93.7 1.4 copy-done.1
  95.1 1.1 copy-done.2
  96.2 1.0 copy-done.3
  97.2 1.0 copy-done.4
  98.3 0.9 copy-done.5
  99.2 0.9 copy-done.6
  100.2 0.7 copy-done.7
  100.9 0.7 copy-done.9
  101.6 0.7 copy-done.10
  102.2 52.4 %main.1 = (f32[4,256,512]{2,1,0:T(8,128)}, f32[1024,16,128]{2,1,0:T(8,128)}) custom-call(s32[2]{0:T(128)S(1)} %copy-done.8, bf16[8,4,32,768]{3,2,1,0:T(8,128)(2,1)S(1)} %bitcast.7, bf16[2,8,4,32,768]{4,3,2,1,0:T(8,128)(2,1)} %bitcast.8, bf16[512,768]{1,0:T(8,128)(2,1)S(1)} %copy-done.2, bf16[512,512]{1,0:T(8,128)(2,1)S(1)} %copy-done.3, ...), custom_call_target="tpu_custom_call" | custom-call | tf_op jit(solution)/shard_map/main/pallas_call | solution.py:445
  (15 shorter events, 0.0 us)
Async XLA Ops:
  7.2 79.2 %all-gather.5.cloned.1.call-start = ((), (), s32[]{:S(2)}) async-start(), calls=%async_computation.2 | async-start | bytes 1769472 | tf_op jit(solution)/shard_map/all_gather | solution.py:488
  9.6 18.2 %all-to-all-start = ((bf16[16,2,8,768]{3,2,1,0:T(8,128)(2,1)}), bf16[16,2,8,768]{3,2,1,0:T(8,128)(2,1)S(1)}, u32[]{:S(2)}, u32[]{:S(2)}) async-start(bf16[16,2,8,768]{3,2,1,0:T(8,128)(2,1)} %choose.1), calls=%async_computation | async-start | bytes 786432 | tf_op jit(solution)/shard_map/all_to_all | solution.py:476
  17.8 74.5 %all-gather.7.cloned.1.call-start = ((), (), s32[]{:S(2)}) async-start(), calls=%async_computation.3 | async-start | bytes 3342336 | tf_op jit(solution)/shard_map/all_gather | solution.py:493
  17.8 1.6 collective-permute-start
  19.4 8.5 %copy-start.13 = (bf16[4,32,768]{2,1,0:T(8,128)(2,1)}, bf16[4,32,768]{2,1,0:T(8,128)(2,1)S(1)}, u32[]{:S(2)}) copy-start(bf16[4,32,768]{2,1,0:T(8,128)(2,1)S(1)} %collective-permute-done) | copy-start | bytes 589828
  27.8 0.7 copy-start.11
  57.7 1.7 %copy-start.12 = (bf16[16,2,8,768]{3,2,1,0:T(8,128)(2,1)}, bf16[16,2,8,768]{3,2,1,0:T(8,128)(2,1)S(1)}, u32[]{:S(2)}) copy-start(bf16[16,2,8,768]{3,2,1,0:T(8,128)(2,1)S(1)} %all_to_all.10.mine) | copy-start | bytes 1179652
  57.7 34.6 %copy-start.8 = (s32[2]{0:T(128)S(1)}, s32[2]{0:T(128)}, u32[]{:S(2)}) copy-start(s32[2]{0:T(128)} %order.5) | copy-start | bytes 28
  57.7 1.7 %collective-permute-start.1 = (bf16[16,2,8,768]{3,2,1,0:T(8,128)(2,1)S(1)}, bf16[16,2,8,768]{3,2,1,0:T(8,128)(2,1)S(1)}, u32[]{:S(2)}, u32[]{:S(2)}) collective-permute-start(bf16[16,2,8,768]{3,2,1,0:T(8,128)(2,1)S(1)} %all_to_all.10.mine), channel_id=1, source_target_pairs={{0,1},{1,0},{2,3},{3,2},{4,5},{5,4},{6,7},{7,6},{8,9},{9,8},{10,11... | collective-permute-start | bytes 1179656 | tf_op jit(solution)/shard_map/ppermute | solution.py:500
  59.4 0.8 copy-start.14
  92.2 1.4 copy-start
  93.6 1.4 copy-start.1
  95.1 1.1 copy-start.2
  96.2 1.0 copy-start.3
  97.2 1.0 copy-start.4
  98.3 0.9 copy-start.5
  99.2 0.9 copy-start.6
  100.2 0.7 copy-start.7
  100.9 0.7 copy-start.9
  101.6 0.7 copy-start.10
Sparse Core Ops, SparseCore 0:
  9.7 32.0 all-gather.4
  43.9 48.2 all-gather.6
